TPU v7x, 32 devices: a whole 2x2x4 slice. The times are simulated.
32 devices in a mesh: seq: 8 (over z, core), fsdp: 4 (over y, x).
Axes of the slice: x: 2, y: 2, z: 4, core: 2. Of those that a mesh axis runs over, the one named last changes fastest.
Arguments:
- hidden: bfloat16 [4, 1280, 2048], P('fsdp', 'seq'), may hold values from -6 to 6
- lengths: int32 [4, 4], replicated, may hold values from 1 to 1024, 1280 in all within a row
- w_input: bfloat16 [2048, 2048], P(None, 'fsdp'), may hold values from -0.125 to 0.125
- w_forget: bfloat16 [2048, 2048], P(None, 'fsdp'), may hold values from -0.125 to 0.125
- w_gate_out: bfloat16 [2048, 2048], P(None, 'fsdp'), may hold values from -0.125 to 0.125
- w_output: bfloat16 [2048, 2048], P('fsdp'), may hold values from -0.25 to 0.25
- norm_gain: float32 [2048], replicated, may hold values from 0.5 to 1.5
- gate_gain: float32 [2048], replicated, may hold values from 0.5 to 1.5
- glu_gain: float32 [2048], replicated, may hold values from 0.5 to 1.5
- lower_table: float32 [24, 2048], replicated, may hold values from -12 to 12
- w_glu_gate: bfloat16 [2048, 5632], P(None, 'fsdp'), may hold values from -0.125 to 0.125
- w_glu_up: bfloat16 [2048, 5632], P(None, 'fsdp'), may hold values from -0.125 to 0.125
- w_glu_down: bfloat16 [5632, 2048], P('fsdp'), may hold values from -0.15625 to 0.15625
- cotangent: bfloat16 [4, 1280, 2048], P('fsdp', 'seq'), may hold values from -6 to 6
Outputs:
- output: bfloat16 [4, 1280, 2048], P('fsdp', 'seq')
- grad_hidden: bfloat16 [4, 1280, 2048], P('fsdp', 'seq')
- grad_w_input: float32 [2048, 2048], P('seq', 'fsdp')
- grad_w_forget: float32 [2048, 2048], P('seq', 'fsdp')
- grad_w_gate_out: float32 [2048, 2048], P('seq', 'fsdp')
- grad_w_output: float32 [2048, 2048], P('fsdp', 'seq')
- grad_norm_gain: float32 [2048], replicated
- grad_gate_gain: float32 [2048], replicated
- grad_glu_gain: float32 [2048], replicated
- grad_lower_table: float32 [24, 2048], replicated
- grad_glu_gate: float32 [2048, 5632], P('seq', 'fsdp')
- grad_glu_up: float32 [2048, 5632], P('seq', 'fsdp')
- grad_glu_down: float32 [5632, 2048], P('fsdp', 'seq')
Inputs may be any that keep to these rules, and one draw needn't show every extreme that they name: Each row holds the lengths of one group's 4 sequences; they sum to 1280 and the largest is 1024.
All inputs are finite; a program needn't handle non-finite values.
Results may differ from a plain program's by a relative error of at most 0.017.
Values may be sent and summed in bfloat16 or wider, within the bound.
A program may use at most 256 MiB of HBM per device.

v0:
```python
import functools

import jax
import jax.numpy as jnp
from jax import lax
from jax.experimental import pallas as pl
from jax.experimental.pallas import tpu as pltpu
from jax.sharding import PartitionSpec as P

LAYER = 12
MESH = pl.DeviceIdType.MESH
F32 = jnp.float32
BF16 = jnp.bfloat16

epsilon = 1e-06

VMEM = pl.BlockSpec(memory_space=pltpu.VMEM)
ANY = pl.BlockSpec(memory_space=pl.ANY)


def lower_bound(table):
    soft = jax.nn.softmax(table, axis=0)
    totals = jnp.cumsum(soft, axis=0)
    return totals[LAYER] - totals[0]


def silu_slope(value, sigma):
    return sigma * (1.0 + value * (1.0 - sigma))


def params(collective_id):
    return pltpu.CompilerParams(
        collective_id=collective_id, has_side_effects=True, vmem_limit_bytes=56 << 20
    )


def round_up(value, unit):
    return -(-value // unit) * unit


def plane():
    s = lax.axis_index("seq")
    f = lax.axis_index("fsdp")
    y, x = f // 2, f % 2
    fx = y * 2 + (1 - x)
    fy = (1 - y) * 2 + x
    fd = (1 - y) * 2 + (1 - x)
    return s, f, fx, fy, fd


def enter(devices):
    barrier = pltpu.get_barrier_semaphore()
    for device in devices:
        pl.semaphore_signal(barrier, inc=1, device_id=device, device_id_type=MESH)
    pl.semaphore_wait(barrier, len(devices))


def remote(src, dst, send, recv, device):
    return pltpu.make_async_remote_copy(
        src_ref=src,
        dst_ref=dst,
        send_sem=send,
        recv_sem=recv,
        device_id=device,
        device_id_type=MESH,
    )


def gather(x, small, collective_id):
    return lax.all_gather(x, "fsdp"), lax.all_gather(small, "fsdp")


def reduce_rows(p, small, collective_id):
    total = lax.psum_scatter(p, "fsdp", scatter_dimension=0, tiled=True)[0]
    return total.astype(F32), lax.psum(small, "fsdp")


def start_exchange(total, gathered, send, recv, n_seq):
    s = lax.axis_index("seq")
    f = lax.axis_index("fsdp")
    copies = []
    for k in range(1, n_seq):
        peer = lax.rem(s + k, n_seq)
        copy = remote(total, gathered.at[s], send.at[k], recv.at[k], (peer, f))
        copy.start()
        copies.append(copy)
    gathered[pl.ds(s, 1)] = total[...][None]
    return copies


def seq_peers(n_seq):
    s = lax.axis_index("seq")
    f = lax.axis_index("fsdp")
    return [(lax.rem(s + k, n_seq), f) for k in range(1, n_seq)]


def lane_blocks(groups, chans):
    return [(g, slice(c, c + 128)) for g in range(groups) for c in range(0, chans, 128)]


def forward_scan_kernel(
    n_seq, in_raw, forget_raw, bounds, keep, state_b, before, a_ref, b_ref, total, gathered, send, recv
):
    groups, rows, chans = in_raw.shape
    part = rows // 8
    blocks = lane_blocks(groups, chans)
    s = lax.axis_index("seq")
    barrier = pltpu.get_barrier_semaphore()
    for peer in seq_peers(n_seq):
        pl.semaphore_signal(barrier, inc=1, device_id=peer, device_id_type=MESH)
    for n, (g, lanes) in enumerate(blocks):
        bound = bounds[:, lanes]
        forget = bound + (1.0 - bound) * jax.nn.sigmoid(forget_raw[g, :, lanes].astype(F32))
        value = in_raw[g, :, lanes].astype(F32)
        a_ref[n] = forget * keep[g]
        b_ref[n] = value * jax.nn.sigmoid(value) * (1.0 - forget)

    def step(i, carry):
        new = []
        at = pl.ds(i, 8, stride=part)
        for n, (product, state) in enumerate(carry):
            a = a_ref[n, at, :]
            state = a * state + b_ref[n, at, :]
            product = product * a
            a_ref[n, at, :] = product
            b_ref[n, at, :] = state
            new.append((product, state))
        return tuple(new)

    start = tuple((jnp.ones((8, 128), F32), jnp.zeros((8, 128), F32)) for _ in blocks)
    ends = lax.fori_loop(0, part, step, start)
    for n, (product, state) in enumerate(ends):
        p_all, s_all = product[0:1], state[0:1]
        for j in range(1, 8):
            p_all, s_all = p_all * product[j : j + 1], state[j : j + 1] + product[j : j + 1] * s_all
        total[2 * n : 2 * n + 1] = p_all
        total[2 * n + 1 : 2 * n + 2] = s_all
    pl.semaphore_wait(barrier, n_seq - 1)
    copies = start_exchange(total, gathered, send, recv, n_seq)
    for copy in copies:
        copy.wait()
    for n, (g, lanes) in enumerate(blocks):
        carry = jnp.zeros((1, 128), F32)
        for j in range(n_seq - 1):
            p_j = gathered[j, 2 * n : 2 * n + 1]
            s_j = gathered[j, 2 * n + 1 : 2 * n + 2]
            carry = jnp.where(j < s, s_j + p_j * carry, carry)
        before[g, 0:1, lanes] = carry
        product, state = ends[n]
        carries = [carry]
        for j in range(7):
            carries.append(state[j : j + 1] + product[j : j + 1] * carries[-1])
        for j in range(8):
            at = slice(j * part, (j + 1) * part)
            b_ref[n, at] = b_ref[n, at] + a_ref[n, at] * carries[j]
        state_b[g, :, lanes] = b_ref[n].astype(BF16)
        before[g, 1:rows, lanes] = b_ref[n, 0 : rows - 1]


def forward_scan(in_raw, forget_raw, bounds, keep, collective_id):
    n_seq = lax.axis_size("seq")
    groups, rows, chans = in_raw.shape
    blocks = groups * chans // 128
    return pl.pallas_call(
        functools.partial(forward_scan_kernel, n_seq),
        out_shape=(
            jax.ShapeDtypeStruct(in_raw.shape, BF16),
            jax.ShapeDtypeStruct(in_raw.shape, F32),
        ),
        in_specs=[VMEM] * 4,
        out_specs=(VMEM, VMEM),
        scratch_shapes=[
            pltpu.VMEM((blocks, rows, 128), F32),
            pltpu.VMEM((blocks, rows, 128), F32),
            pltpu.VMEM((2 * blocks, 128), F32),
            pltpu.VMEM((n_seq, 2 * blocks, 128), F32),
            pltpu.SemaphoreType.DMA((n_seq,)),
            pltpu.SemaphoreType.DMA((n_seq,)),
        ],
        compiler_params=params(collective_id),
        name="forward_scan",
    )(in_raw, forget_raw, bounds, keep)


def backward_scan_kernel(
    n_seq,
    d_state,
    in_raw,
    forget_raw,
    before,
    bounds,
    keep,
    d_in,
    d_forget_raw,
    d_bounds,
    p_ref,
    q_ref,
    total,
    gathered,
    send,
    recv,
):
    groups, rows, chans = in_raw.shape
    part = rows // 8
    blocks = lane_blocks(groups, chans)
    s = lax.axis_index("seq")
    barrier = pltpu.get_barrier_semaphore()
    for peer in seq_peers(n_seq):
        pl.semaphore_signal(barrier, inc=1, device_id=peer, device_id_type=MESH)
    for n, (g, lanes) in enumerate(blocks):
        bound = bounds[:, lanes]
        forget = bound + (1.0 - bound) * jax.nn.sigmoid(forget_raw[g, :, lanes].astype(F32))
        p_ref[n] = forget * keep[g]
        q_ref[n] = d_state[g, :, lanes].astype(F32)

    def step(i, carry):
        new = []
        at = pl.ds(part - 1 - i, 8, stride=part)
        for n, (product, message) in enumerate(carry):
            a = p_ref[n, at, :]
            acc = q_ref[n, at, :] + message
            p_ref[n, at, :] = product
            q_ref[n, at, :] = acc
            new.append((product * a, a * acc))
        return tuple(new)

    start = tuple((jnp.ones((8, 128), F32), jnp.zeros((8, 128), F32)) for _ in blocks)
    ends = lax.fori_loop(0, part, step, start)
    for n, (product, message) in enumerate(ends):
        p_all, m_all = product[7:8], message[7:8]
        for j in range(6, -1, -1):
            p_all, m_all = p_all * product[j : j + 1], message[j : j + 1] + product[j : j + 1] * m_all
        total[2 * n : 2 * n + 1] = p_all
        total[2 * n + 1 : 2 * n + 2] = m_all
    pl.semaphore_wait(barrier, n_seq - 1)
    copies = start_exchange(total, gathered, send, recv, n_seq)
    for copy in copies:
        copy.wait()
    d_bounds[...] = jnp.zeros((1, chans), F32)
    for n, (g, lanes) in enumerate(blocks):
        carry = jnp.zeros((1, 128), F32)
        for j in range(n_seq - 1, 0, -1):
            p_j = gathered[j, 2 * n : 2 * n + 1]
            m_j = gathered[j, 2 * n + 1 : 2 * n + 2]
            carry = jnp.where(j > s, m_j + p_j * carry, carry)
        product, message = ends[n]
        carries = [carry]
        for j in range(7, 0, -1):
            carries.append(message[j : j + 1] + product[j : j + 1] * carries[-1])
        carries = carries[::-1]
        for j in range(8):
            at = slice(j * part, (j + 1) * part)
            q_ref[n, at] = q_ref[n, at] + p_ref[n, at] * carries[j]
        acc = q_ref[n]
        bound = bounds[:, lanes]
        sigma_f = jax.nn.sigmoid(forget_raw[g, :, lanes].astype(F32))
        forget = bound + (1.0 - bound) * sigma_f
        value = in_raw[g, :, lanes].astype(F32)
        sigma_i = jax.nn.sigmoid(value)
        d_forget = acc * (before[g, :, lanes] * keep[g] - value * sigma_i)
        d_in[g, :, lanes] = (acc * (1.0 - forget) * silu_slope(value, sigma_i)).astype(BF16)
        d_sigma = d_forget * (1.0 - sigma_f)
        d_forget_raw[g, :, lanes] = (d_sigma * (1.0 - bound) * sigma_f).astype(BF16)
        d_bounds[:, lanes] += jnp.sum(d_sigma, 0, keepdims=True)


def backward_scan(d_state, in_raw, forget_raw, before, bounds, keep, collective_id):
    n_seq = lax.axis_size("seq")
    groups, rows, chans = in_raw.shape
    blocks = groups * chans // 128
    return pl.pallas_call(
        functools.partial(backward_scan_kernel, n_seq),
        out_shape=(
            jax.ShapeDtypeStruct(in_raw.shape, BF16),
            jax.ShapeDtypeStruct(in_raw.shape, BF16),
            jax.ShapeDtypeStruct((1, chans), F32),
        ),
        in_specs=[VMEM] * 6,
        out_specs=(VMEM, VMEM, VMEM),
        scratch_shapes=[
            pltpu.VMEM((blocks, rows, 128), F32),
            pltpu.VMEM((blocks, rows, 128), F32),
            pltpu.VMEM((2 * blocks, 128), F32),
            pltpu.VMEM((n_seq, 2 * blocks, 128), F32),
            pltpu.SemaphoreType.DMA((n_seq,)),
            pltpu.SemaphoreType.DMA((n_seq,)),
        ],
        compiler_params=params(collective_id),
        name="backward_scan",
    )(d_state, in_raw, forget_raw, before, bounds, keep)


def sum_all_kernel(n_seq, n_fsdp, x, out, middle, over_seq, over_fsdp, send, recv):
    s = lax.axis_index("seq")
    f = lax.axis_index("fsdp")
    along = [(lax.rem(s + k, n_seq), f) for k in range(1, n_seq)]
    across = [(s, lax.rem(f + k, n_fsdp)) for k in range(1, n_fsdp)]
    enter(along + across)
    copies = []
    for k, peer in enumerate(along):
        copy = remote(x, over_seq.at[k], send.at[k], recv.at[k], peer)
        copy.start()
        copies.append(copy)
    total = x[...]
    for k, copy in enumerate(copies):
        copy.wait_recv()
        total = total + over_seq[k]
    middle[...] = total
    later = []
    for k, peer in enumerate(across):
        slot = n_seq - 1 + k
        copy = remote(middle, over_fsdp.at[k], send.at[slot], recv.at[slot], peer)
        copy.start()
        later.append(copy)
    for k, copy in enumerate(later):
        copy.wait_recv()
        total = total + over_fsdp[k]
    out[...] = total
    for copy in copies + later:
        copy.wait_send()


def sum_all(x, collective_id):
    n_seq, n_fsdp = lax.axis_size("seq"), lax.axis_size("fsdp")
    count = n_seq + n_fsdp - 2
    return pl.pallas_call(
        functools.partial(sum_all_kernel, n_seq, n_fsdp),
        out_shape=jax.ShapeDtypeStruct(x.shape, F32),
        in_specs=[VMEM],
        out_specs=VMEM,
        scratch_shapes=[
            pltpu.VMEM(x.shape, F32),
            pltpu.VMEM((n_seq - 1,) + x.shape, F32),
            pltpu.VMEM((n_fsdp - 1,) + x.shape, F32),
            pltpu.SemaphoreType.DMA((count,)),
            pltpu.SemaphoreType.DMA((count,)),
        ],
        compiler_params=params(collective_id),
        name="sum_all",
    )(x)


def sum_over_seq(part):
    return lax.psum_scatter(part.astype(BF16), "seq", scatter_dimension=0, tiled=True).astype(F32)


def per_device(
    hidden,
    lengths,
    w_input,
    w_forget,
    w_gate_out,
    w_output,
    norm_gain,
    gate_gain,
    glu_gain,
    lower_table,
    w_glu_gate,
    w_glu_up,
    w_glu_down,
    cotangent,
):
    seq_index = lax.axis_index("seq")
    fsdp_index = lax.axis_index("fsdp")
    groups = lax.axis_size("fsdp")
    _, rows, width = hidden.shape
    chans = w_input.shape[1]
    units = w_glu_gate.shape[1]
    tokens = groups * rows
    small_shape = (round_up(groups, 8), round_up(rows, 128))

    def to_small(value):
        return jnp.pad(
            value, ((0, small_shape[0] - value.shape[0]), (0, small_shape[1] - value.shape[1]))
        )

    def dot(left, right):
        return jnp.dot(left, right, preferred_element_type=F32)

    def dot_t(left, right):
        return lax.dot_general(left, right, (((1,), (1,)), ((), ())), preferred_element_type=F32)

    def over_tokens(left, right):
        return lax.dot_general(left, right, (((0,), (0,)), ((), ())), preferred_element_type=F32)

    cotangent_all = lax.all_gather(cotangent[0], "fsdp").reshape(tokens, width)

    hidden_f = hidden[0].astype(F32)
    scale_one = lax.rsqrt(jnp.mean(hidden_f * hidden_f, -1, keepdims=True) + epsilon)
    normed = (hidden_f * scale_one * norm_gain).astype(BF16)
    normed_all, _ = gather(normed, jnp.zeros((8, 128), F32), 0)
    normed_all = normed_all.reshape(tokens, width)
    in_raw = dot(normed_all, w_input).astype(BF16).reshape(groups, rows, chans)
    forget_raw = dot(normed_all, w_forget).astype(BF16).reshape(groups, rows, chans)
    gate_raw = dot(normed_all, w_gate_out)

    bounds_full = lower_bound(lower_table)
    bounds = lax.dynamic_slice_in_dim(bounds_full, fsdp_index * chans, chans)[None]
    seq_starts = jnp.cumsum(lengths, axis=1) - lengths
    places = seq_index * rows + jnp.arange(rows, dtype=jnp.int32)
    starts = jnp.any(places[None, :, None] == seq_starts[:, None, :], axis=-1)
    keep = jnp.where(starts, 0.0, 1.0).astype(F32)[:, :, None]
    state_b, before = forward_scan(in_raw, forget_raw, bounds, keep, 1)

    state_f = state_b.astype(F32).reshape(tokens, chans)
    gain_slice = lax.dynamic_slice_in_dim(gate_gain, fsdp_index * chans, chans)
    sigma_g = jax.nn.sigmoid(gate_raw)
    silu_gate = gate_raw * sigma_g
    out_raw = (state_f * gain_slice * silu_gate).astype(BF16)
    squares = jnp.sum(state_f * state_f, -1).reshape(groups, rows)
    mixed_part = dot(out_raw, w_output).astype(BF16).reshape(groups, rows, width)
    mixed_raw, square_sum = reduce_rows(mixed_part, to_small(squares), 2)
    state_scale = lax.rsqrt(square_sum[:groups, :rows] / width + epsilon)
    own_scale = lax.dynamic_slice_in_dim(state_scale, fsdp_index, 1, 0)[0][:, None]
    scale_g = state_scale.reshape(tokens, 1)
    middle = hidden_f + own_scale * mixed_raw
    scale_two = lax.rsqrt(jnp.mean(middle * middle, -1, keepdims=True) + epsilon)
    normed_two = (middle * scale_two * glu_gain).astype(BF16)
    normed_two_all, _ = gather(normed_two, jnp.zeros((8, 128), F32), 3)
    normed_two_all = normed_two_all.reshape(tokens, width)

    gate_val = dot(normed_two_all, w_glu_gate)
    up_val = dot(normed_two_all, w_glu_up)
    sigma_u = jax.nn.sigmoid(gate_val)
    silu_u = gate_val * sigma_u
    activity = (silu_u * up_val).astype(BF16)
    down_grad = sum_over_seq(over_tokens(cotangent_all, activity))
    d_act = dot_t(cotangent_all, w_glu_down)
    d_gate = (d_act * up_val * silu_slope(gate_val, sigma_u)).astype(BF16)
    d_up = (d_act * silu_u).astype(BF16)
    pair_grad = sum_over_seq(
        jnp.concatenate(
            [
                over_tokens(normed_two_all, d_gate).astype(BF16),
                over_tokens(normed_two_all, d_up).astype(BF16),
            ],
            1,
        )
    )
    d_two_part = (dot_t(d_gate, w_glu_gate) + dot_t(d_up, w_glu_up)).astype(BF16)
    no_small = jnp.zeros((8, 128), F32)
    d_normed_two, _ = reduce_rows(d_two_part.reshape(groups, rows, width), no_small, 4)
    glu_part = dot(activity, w_glu_down).astype(BF16).reshape(groups, rows, width)
    glu_result = lax.psum_scatter(glu_part, "fsdp", scatter_dimension=0, tiled=True)[0]
    output = (middle + glu_result.astype(F32)).astype(BF16)[None]

    cotangent_f = cotangent[0].astype(F32)
    scaled_two = glu_gain * d_normed_two
    d_middle = (
        cotangent_f
        + scale_two * scaled_two
        - middle * scale_two**3 * jnp.mean(scaled_two * middle, -1, keepdims=True)
    )
    d_glu_gain = jnp.sum(d_normed_two * middle * scale_two, 0)
    d_mixed = d_middle.astype(BF16)
    own_dot = jnp.sum(d_mixed.astype(F32) * mixed_raw, -1)[None]
    d_mixed_all, dots = gather(d_mixed, to_small(own_dot), 5)
    d_mixed_all = d_mixed_all.reshape(tokens, width)
    dot_rows = dots[:, 0, :rows].reshape(tokens, 1)

    d_out = dot_t(d_mixed_all, w_output)
    scaled_state = state_f * scale_g
    d_gain_slice = jnp.sum(d_out * scaled_state * silu_gate, 0)
    d_scaled = d_out * gain_slice * silu_gate
    d_gate_raw = (d_out * scaled_state * gain_slice * silu_slope(gate_raw, sigma_g)).astype(BF16)
    d_state = scale_g * d_scaled - state_f * (scale_g**3 * (dot_rows / width))
    d_state = d_state.astype(BF16).reshape(groups, rows, chans)
    d_in, d_forget_raw, d_bounds = backward_scan(
        d_state, in_raw, forget_raw, before, bounds, keep, 6
    )
    d_in = d_in.reshape(tokens, chans)
    d_forget_raw = d_forget_raw.reshape(tokens, chans)

    d_normed_part = dot_t(d_in, w_input) + dot_t(d_forget_raw, w_forget)
    d_normed_part = (d_normed_part + dot_t(d_gate_raw, w_gate_out)).astype(BF16)
    out_gate = (out_raw.astype(F32) * scale_g).astype(BF16)
    mixer_grad = sum_over_seq(
        jnp.concatenate(
            [
                over_tokens(d_mixed_all, out_gate).astype(BF16),
                over_tokens(normed_all, d_in).astype(BF16),
                over_tokens(normed_all, d_forget_raw).astype(BF16),
                over_tokens(normed_all, d_gate_raw).astype(BF16),
            ],
            1,
        )
    )
    d_normed, _ = reduce_rows(d_normed_part.reshape(groups, rows, width), no_small, 7)
    scaled_one = norm_gain * d_normed
    d_hidden = (
        d_middle
        + scale_one * scaled_one
        - hidden_f * scale_one**3 * jnp.mean(scaled_one * hidden_f, -1, keepdims=True)
    )
    d_norm_gain = jnp.sum(d_normed * hidden_f * scale_one, 0)
    d_gain_full = lax.dynamic_update_slice(
        jnp.zeros((width,), F32), d_gain_slice, (fsdp_index * chans,)
    )
    d_bounds_full = lax.dynamic_update_slice(
        jnp.zeros((width,), F32), d_bounds[0], (fsdp_index * chans,)
    )
    sums = jnp.stack([d_norm_gain, d_glu_gain, d_gain_full, d_bounds_full])
    totals = sum_all(sums.reshape(8, width // 2), 8).reshape(4, width)
    _, bounds_pull = jax.vjp(lower_bound, lower_table)
    d_table = bounds_pull(totals[3])[0]
    return (
        output,
        d_hidden.astype(BF16)[None],
        mixer_grad[:, chans : 2 * chans],
        mixer_grad[:, 2 * chans : 3 * chans],
        mixer_grad[:, 3 * chans :],
        mixer_grad[:, :chans].T,
        totals[0],
        totals[2],
        totals[1],
        d_table,
        pair_grad[:, :units],
        pair_grad[:, units:],
        down_grad.T,
    )


def copy_in(src, dst, sem):
    copy = pltpu.make_async_copy(src, dst, sem)
    copy.start()
    return copy


class Links:
    def __init__(self, send, recv):
        self.send, self.recv, self.used = send, recv, 0

    def start(self, src, dst, device):
        copy = remote(src, dst, self.send.at[self.used], self.recv.at[self.used], device)
        self.used += 1
        copy.start()
        return copy


class Locals:
    def __init__(self, sems):
        self.sems, self.used = sems, 0

    def start(self, src, dst):
        copy = copy_in(src, dst, self.sems.at[self.used])
        self.used += 1
        return copy


def row_slots(rows):
    half = rows // 2
    top = [pl.ds(k * rows, half) for k in range(4)]
    bottom = [pl.ds(k * rows + half, half) for k in range(4)]
    return top, bottom


def gather_start(links, src, dst, rows, s, fx, fy):
    half = rows // 2
    top, bottom = row_slots(rows)
    here = (pl.ds(0, half), pl.ds(half, half))
    return [
        links.start(src.at[here[0]], dst.at[top[1]], (s, fx)),
        links.start(src.at[here[1]], dst.at[bottom[2]], (s, fy)),
        links.start(src.at[here[1]], dst.at[bottom[1]], (s, fx)),
        links.start(src.at[here[0]], dst.at[top[2]], (s, fy)),
    ]


def gather_forward(links, own, dst, rows, s, fx, fy):
    top, bottom = row_slots(rows)
    own[0].wait_recv()
    on_y = links.start(dst.at[top[1]], dst.at[top[3]], (s, fy))
    own[1].wait_recv()
    on_x = links.start(dst.at[bottom[2]], dst.at[bottom[3]], (s, fx))
    return [on_y, on_x]


def gather_middle(own):
    own[2].wait_recv()
    own[3].wait_recv()


def gather_far(later):
    for copy in later:
        copy.wait_recv()


def sends_done(*lists):
    for copies in lists:
        for copy in copies:
            copy.wait_send()


def wait_all(*lists):
    for copies in lists:
        for copy in copies:
            copy.wait()


def reduce_start_far(links, part, from_x, from_y, rows, s, fx, fy):
    top, bottom = row_slots(rows)
    return [
        links.start(part.at[top[3]], from_x.at[0], (s, fx)),
        links.start(part.at[bottom[3]], from_y.at[0], (s, fy)),
    ]


def reduce_start_near(links, part, from_x, from_y, rows, s, fx, fy):
    top, bottom = row_slots(rows)
    return [
        links.start(part.at[top[1]], from_x.at[1], (s, fx)),
        links.start(part.at[bottom[2]], from_y.at[1], (s, fy)),
    ]


def reduce_pass(links, far, part, from_x, from_y, pass_x, pass_y, rows, s, fx, fy):
    top, bottom = row_slots(rows)
    far[0].wait_recv()
    pass_y[...] = (from_x[0].astype(F32) + part[top[2]].astype(F32)).astype(BF16)
    on_y = links.start(pass_y, from_y.at[2], (s, fy))
    far[1].wait_recv()
    pass_x[...] = (from_y[0].astype(F32) + part[bottom[1]].astype(F32)).astype(BF16)
    on_x = links.start(pass_x, from_x.at[2], (s, fx))
    return [on_y, on_x]


def mm(left, right):
    return jnp.dot(left, right, preferred_element_type=F32)


def mm_t(left, right):
    return lax.dot_general(left, right, (((1,), (1,)), ((), ())), preferred_element_type=F32)


def tile(n, width):
    return pl.ds(pl.multiple_of(n * width, width), width)


def bounds_slice(table, first, count):
    rows = table[:, pl.ds(pl.multiple_of(first, 128), count)]
    powers = jnp.exp(rows - jnp.max(rows, 0, keepdims=True))
    return jnp.sum(powers[1 : LAYER + 1], 0, keepdims=True) / jnp.sum(powers, 0, keepdims=True)


def keep_rows(lengths, group, first, rows):
    places = first + lax.broadcasted_iota(jnp.int32, (rows, 128), 0)
    start = jnp.int32(0)
    keep = jnp.where(places == start, 0.0, 1.0)
    for i in range(lengths.shape[1] - 1):
        start = start + lengths[group, i]
        keep = jnp.where(places == start, 0.0, keep)
    return keep.astype(F32)


def segment_totals(end_p, end_s, blocks, order):
    first, rest = order[0], order[1:]
    p_all = end_p[pl.ds(first, blocks, stride=8), :]
    s_all = end_s[pl.ds(first, blocks, stride=8), :]
    for j in rest:
        p_j = end_p[pl.ds(j, blocks, stride=8), :]
        s_all = end_s[pl.ds(j, blocks, stride=8), :] + p_j * s_all
        p_all = p_all * p_j
    return p_all, s_all


def spread_carry(carry, carr, end_p, end_s, blocks, order):
    for i, j in enumerate(order):
        carr[pl.ds(j, blocks, stride=8), :] = carry
        if i < 7:
            carry = end_s[pl.ds(j, blocks, stride=8), :] + end_p[pl.ds(j, blocks, stride=8), :] * carry


def mixer_kernel(
    n_seq,
    lengths,
    hidden,
    cot,
    norm_gain,
    gate_gain,
    glu_gain,
    table,
    w_in,
    w_fg,
    w_gt,
    w_out,
    normed_half,
    cot_out,
    in_out,
    fg_out,
    gate_out,
    state_out,
    raw_out,
    before_out,
    scale_out,
    middle,
    two,
    wv,
    wo,
    rows_all,
    stage,
    in_ref,
    fg_ref,
    gate_ref,
    a_ref,
    b_ref,
    shifted,
    keep_ref,
    end_p,
    end_s,
    carr,
    total,
    gathered,
    state_ref,
    raw_ref,
    squares,
    squares_t,
    packed,
    squares_in,
    part,
    from_x,
    from_y,
    pass_x,
    pass_y,
    send,
    recv,
    exchange_send,
    exchange_recv,
    local_sems,
):
    rows, width = hidden.shape
    chans = w_in.shape[1]
    lanes_of = [slice(c, c + 128) for c in range(0, chans, 128)]
    count = len(lanes_of)
    blocks = 4 * count
    step_len = rows // 8
    s, f, fx, fy, fd = plane()
    groups = [f, fx, fy, fd]
    links, local = Links(send, recv), Locals(local_sems)

    weights = [
        local.start(w, wv.at[:, pl.ds(i * chans, chans)]) for i, w in enumerate((w_in, w_fg, w_gt))
    ]
    weights.append(local.start(w_out, wo))
    barrier = pltpu.get_barrier_semaphore()
    peers = [(s, fx), (s, fy), (s, fd)] + seq_peers(n_seq)
    for peer in peers:
        pl.semaphore_signal(barrier, inc=1, device_id=peer, device_id_type=MESH)

    def norm_rows(i, _):
        at = pl.ds(pl.multiple_of(i * 16, 16), 16)
        value = hidden[at].astype(F32)
        scale = lax.rsqrt(jnp.mean(value * value, -1, keepdims=True) + epsilon)
        rows_all[at] = (value * scale * norm_gain[...]).astype(BF16)
        return 0

    lax.fori_loop(0, rows // 16, norm_rows, 0)
    pl.semaphore_wait(barrier, len(peers))
    own = gather_start(links, rows_all, rows_all, rows, s, fx, fy)
    bound = bounds_slice(table, f * chans, chans)
    for k in range(4):
        keep_ref[k] = keep_rows(lengths, groups[k], s * rows, rows)
    squares[...] = jnp.zeros_like(squares)
    squares_t[...] = jnp.zeros_like(squares_t)
    for copy in weights[:3]:
        copy.wait()

    def project(first, slots):
        def tile_of(n, _):
            cols = tile(n, 256)
            stage[: slots * rows, cols] = mm(
                rows_all[first * rows : (first + slots) * rows], wv[:, cols]
            )
            return 0

        lax.fori_loop(0, 3 * chans // 256, tile_of, 0)
        for k in range(slots):
            at = slice(k * rows, (k + 1) * rows)
            for c, lanes in enumerate(lanes_of):
                n = (first + k) * count + c
                value = stage[at, lanes].astype(BF16)
                in_ref[first + k, :, lanes] = value
                value = value.astype(F32)
                raw = stage[at, chans + c * 128 : chans + (c + 1) * 128].astype(BF16)
                fg_ref[first + k, :, lanes] = raw
                edge = bound[:, lanes]
                forget = edge + (1.0 - edge) * jax.nn.sigmoid(raw.astype(F32))
                a_ref[n] = forget * keep_ref[first + k]
                b_ref[n] = value * jax.nn.sigmoid(value) * (1.0 - forget)
            gate_ref[first + k] = stage[at, 2 * chans :]

    project(0, 1)
    later = gather_forward(links, own, rows_all, rows, s, fx, fy)
    gather_middle(own)
    project(1, 2)
    gather_far(later)
    cot_own = gather_start(links, cot, cot_out, rows, s, fx, fy)
    core = s % 2
    swaps, outs = swap_columns(
        links, local, rows_all, normed_half, n_seq, core, (s + 1 - 2 * core, f)
    )
    outs.append(local.start(cot, cot_out.at[pl.ds(0, rows)]))
    project(3, 1)
    outs += [
        local.start(in_ref, in_out),
        local.start(fg_ref, fg_out),
        local.start(gate_ref, gate_out),
    ]

    def scan_step(i, carry):
        new = []
        at = pl.ds(i, 8, stride=step_len)
        for n, (product, state) in enumerate(carry):
            a = a_ref[n, at, :]
            state = a * state + b_ref[n, at, :]
            product = product * a
            a_ref[n, at, :] = product
            b_ref[n, at, :] = state
            new.append((product, state))
        return tuple(new)

    start = tuple((jnp.ones((8, 128), F32), jnp.zeros((8, 128), F32)) for _ in range(blocks))
    ends = lax.fori_loop(0, step_len, scan_step, start)
    for n, (product, state) in enumerate(ends):
        end_p[8 * n : 8 * n + 8] = product
        end_s[8 * n : 8 * n + 8] = state
    p_all, s_all = segment_totals(end_p, end_s, blocks, range(8))
    total[:blocks] = p_all
    total[blocks:] = s_all
    copies = start_exchange(total, gathered, exchange_send, exchange_recv, n_seq)
    wait_all(copies)
    carry = jnp.zeros((blocks, 128), F32)
    for j in range(n_seq - 1):
        carry = jnp.where(j < s, gathered[j, blocks:] + gathered[j, :blocks] * carry, carry)
    for n in range(blocks):
        shifted[n, 0:1] = carry[n : n + 1]
    spread_carry(carry, carr, end_p, end_s, blocks, range(8))

    def finish(n, _):
        enter_state = carr[pl.ds(pl.multiple_of(n * 8, 8), 8)]
        for i in range(step_len):
            at = pl.ds(i, 8, stride=step_len)
            state = b_ref[n, at, :] + a_ref[n, at, :] * enter_state
            b_ref[n, at, :] = state
            shifted[n, pl.ds(i + 1, 8, stride=step_len), :] = state
        return 0

    lax.fori_loop(0, blocks, finish, 0)
    outs.append(local.start(shifted.at[:, pl.ds(0, rows)], before_out))

    lane = lax.broadcasted_iota(jnp.int32, (rows, 128), 1)
    for k in (3, 1, 2, 0):
        square = jnp.zeros((rows, 1), F32)
        for c, lanes in enumerate(lanes_of):
            state_b = b_ref[k * count + c].astype(BF16)
            state_ref[k, :, lanes] = state_b
            state = state_b.astype(F32)
            square = square + jnp.sum(state * state, -1, keepdims=True)
            gate = gate_ref[k, :, lanes]
            gain = gate_gain[:, pl.ds(pl.multiple_of(f * chans + c * 128, 128), 128)]
            raw_ref[k * rows : (k + 1) * rows, lanes] = (
                state * gain * gate * jax.nn.sigmoid(gate)
            ).astype(BF16)
        squares[:rows] = jnp.where(lane == groups[k], square, squares[:rows])
    packed[...] = squares[...].T[:8]
    square_copies = [
        links.start(packed, squares_in.at[i], (s, peer)) for i, peer in enumerate((fx, fy, fd))
    ]
    outs += [local.start(state_ref, state_out), local.start(raw_ref, raw_out)]
    cot_later = gather_forward(links, cot_own, cot_out, rows, s, fx, fy)
    weights[3].wait()

    def output_part(first, slots):
        at = slice(first * rows, (first + slots) * rows)

        def tile_of(n, _):
            cols = tile(n, 512)
            part[at, cols] = mm(raw_ref[at], wo[:, cols]).astype(BF16)
            return 0

        lax.fori_loop(0, width // 512, tile_of, 0)

    output_part(3, 1)
    far = reduce_start_far(links, part, from_x, from_y, rows, s, fx, fy)
    output_part(1, 2)
    near = reduce_start_near(links, part, from_x, from_y, rows, s, fx, fy)
    output_part(0, 1)
    passed = reduce_pass(links, far, part, from_x, from_y, pass_x, pass_y, rows, s, fx, fy)
    for copy in square_copies:
        copy.wait_recv()
    all_squares = (packed[...] + squares_in[0]) + (squares_in[1] + squares_in[2])
    squares_t[:8] = lax.rsqrt(all_squares / width + epsilon)
    scales = squares_t[...].T[:rows]
    for k in range(4):
        scale_out[k] = jnp.sum(jnp.where(lane == groups[k], scales, 0.0), -1, keepdims=True)
    for copy in near + passed:
        copy.wait_recv()
    half = rows // 2
    for first, one, other in ((0, from_x.at[1], from_y.at[2]), (half, from_y.at[1], from_x.at[2])):

        def sum_rows(i, _):
            here = pl.ds(pl.multiple_of(i * 16, 16), 16)
            at = pl.ds(pl.multiple_of(first + i * 16, 16), 16)
            mixed = part[at].astype(F32) + one[here].astype(F32) + other[here].astype(F32)
            value = hidden[at].astype(F32) + scale_out[0, at] * mixed
            middle[at] = value
            scale = lax.rsqrt(jnp.mean(value * value, -1, keepdims=True) + epsilon)
            two[at] = (value * scale * glu_gain[...]).astype(BF16)
            return 0

        lax.fori_loop(0, half // 16, sum_rows, 0)
    gather_middle(cot_own)
    gather_far(cot_later)
    sends_done(own, later, cot_own, cot_later, square_copies, far, near, passed)
    wait_all(swaps, outs)


def mixer_forward(lengths, hidden, cot, gains, table, weights, collective_id):
    n_seq = lax.axis_size("seq")
    rows, width = hidden.shape
    chans = weights[0].shape[1]
    blocks = 4 * chans // 128
    tokens = 4 * rows
    half = rows // 2
    shape = jax.ShapeDtypeStruct
    wide = shape((tokens, width), BF16)
    narrow = shape((4, rows, chans), BF16)
    long_rows = round_up(rows, 128)
    return pl.pallas_call(
        functools.partial(mixer_kernel, n_seq),
        out_shape=(
            shape((2, tokens, width // 2), BF16),
            wide,
            narrow,
            narrow,
            shape((4, rows, chans), F32),
            narrow,
            shape((tokens, chans), BF16),
            shape((blocks, rows, 128), F32),
            shape((4, rows, 1), F32),
            shape((rows, width), F32),
            shape((rows, width), BF16),
        ),
        in_specs=[pl.BlockSpec(memory_space=pltpu.SMEM), VMEM, VMEM, VMEM, VMEM, VMEM, VMEM]
        + [ANY] * 4,
        out_specs=(ANY,) * 8 + (VMEM,) * 3,
        scratch_shapes=[
            pltpu.VMEM((width, 3 * chans), BF16),
            pltpu.VMEM((chans, width), BF16),
            pltpu.VMEM((tokens, width), BF16),
            pltpu.VMEM((2 * rows, 3 * chans), F32),
            pltpu.VMEM((4, rows, chans), BF16),
            pltpu.VMEM((4, rows, chans), BF16),
            pltpu.VMEM((4, rows, chans), F32),
            pltpu.VMEM((blocks, rows, 128), F32),
            pltpu.VMEM((blocks, rows, 128), F32),
            pltpu.VMEM((blocks, rows + 8, 128), F32),
            pltpu.VMEM((4, rows, 128), F32),
            pltpu.VMEM((8 * blocks, 128), F32),
            pltpu.VMEM((8 * blocks, 128), F32),
            pltpu.VMEM((8 * blocks, 128), F32),
            pltpu.VMEM((2 * blocks, 128), F32),
            pltpu.VMEM((n_seq, 2 * blocks, 128), F32),
            pltpu.VMEM((4, rows, chans), BF16),
            pltpu.VMEM((tokens, chans), BF16),
            pltpu.VMEM((long_rows, 128), F32),
            pltpu.VMEM((128, long_rows), F32),
            pltpu.VMEM((8, long_rows), F32),
            pltpu.VMEM((3, 8, long_rows), F32),
            pltpu.VMEM((tokens, width), BF16),
            pltpu.VMEM((3, half, width), BF16),
            pltpu.VMEM((3, half, width), BF16),
            pltpu.VMEM((half, width), BF16),
            pltpu.VMEM((half, width), BF16),
            pltpu.SemaphoreType.DMA((21 + n_seq // 2,)),
            pltpu.SemaphoreType.DMA((21 + n_seq // 2,)),
            pltpu.SemaphoreType.DMA((n_seq,)),
            pltpu.SemaphoreType.DMA((n_seq,)),
            pltpu.SemaphoreType.DMA((11 + n_seq // 2,)),
        ],
        compiler_params=params(collective_id),
        name="mixer_forward",
    )(lengths, hidden, cot, *gains, table, *weights)


def swap_columns(links, local, src, dst, n_seq, core, mate):
    part = src.shape[1] // n_seq
    copies, stays = [], []
    for z in range(n_seq // 2):
        to = pl.ds(z * part, part)
        theirs = pl.ds(pl.multiple_of((2 * z + 1 - core) * part, part), part)
        ours = pl.ds(pl.multiple_of((2 * z + core) * part, part), part)
        copies.append(links.start(src.at[:, theirs], dst.at[1, :, to], mate))
        stays.append(local.start(src.at[:, ours], dst.at[0, :, to]))
    return copies, stays


def swap_rows(links, local, src, dst, at, mate):
    copy = links.start(src.at[at], dst.at[1, at], mate)
    return copy, local.start(src.at[at], dst.at[0, at])


def glu_kernel(
    n_seq,
    two,
    cot_all,
    w_gate,
    w_up,
    w_down,
    two_half,
    cot_half,
    act_pair,
    gate_pair,
    up_pair,
    wv,
    wd,
    cot_ref,
    two_ref,
    d_act,
    stage,
    act,
    d_gate,
    d_up,
    send,
    recv,
    local_sems,
):
    rows = two.shape[0]
    units = w_gate.shape[1]
    s, f, fx, fy, fd = plane()
    core = s % 2
    mate = (s + 1 - 2 * core, f)
    links, local = Links(send, recv), Locals(local_sems)
    loads = [
        local.start(w_down, wd),
        local.start(cot_all, cot_ref),
        local.start(w_gate, wv.at[:, pl.ds(0, units)]),
        local.start(w_up, wv.at[:, pl.ds(units, units)]),
    ]
    two_ref[:rows] = two[...]
    enter([(s, fx), (s, fy), mate])
    own = gather_start(links, two_ref, two_ref, rows, s, fx, fy)
    loads[0].wait()
    loads[1].wait()
    swaps, stays = swap_columns(links, local, cot_ref, cot_half, n_seq, core, mate)

    def act_tile(n, _):
        cols = tile(n, 256)
        d_act[:, cols] = mm_t(cot_ref[...], wd[cols])
        return 0

    lax.fori_loop(0, units // 256, act_tile, 0)
    if units % 256:
        rest = slice(units // 256 * 256, units)
        d_act[:, rest] = mm_t(cot_ref[...], wd[rest])
    later = gather_forward(links, own, two_ref, rows, s, fx, fy)
    loads[2].wait()
    loads[3].wait()

    def slots(first, number):
        nonlocal swaps, stays
        base = first * rows

        def tile_of(n, _):
            cols = tile(n, 256)
            stage[: number * rows, cols] = mm(two_ref[base : base + number * rows], wv[:, cols])
            return 0

        lax.fori_loop(0, 2 * units // 256, tile_of, 0)

        def rows_of(i, _):
            at = pl.ds(pl.multiple_of(i * 16, 16), 16)
            to = pl.ds(pl.multiple_of(base + i * 16, 16), 16)
            gate, up = stage[at, :units], stage[at, units:]
            sigma = jax.nn.sigmoid(gate)
            silu = gate * sigma
            act[to] = (silu * up).astype(BF16)
            d = d_act[to]
            d_gate[to] = (d * up * silu_slope(gate, sigma)).astype(BF16)
            d_up[to] = (d * silu).astype(BF16)
            return 0

        lax.fori_loop(0, number * rows // 16, rows_of, 0)
        at = pl.ds(base, number * rows)
        for src, dst in ((act, act_pair), (d_gate, gate_pair), (d_up, up_pair)):
            sent, stayed = swap_rows(links, local, src, dst, at, mate)
            swaps, stays = swaps + [sent], stays + [stayed]

    slots(0, 1)
    gather_middle(own)
    slots(1, 2)
    gather_far(later)
    more, keeps = swap_columns(links, local, two_ref, two_half, n_seq, core, mate)
    slots(3, 1)
    sends_done(own, later)
    wait_all(swaps, stays, more, keeps)


def glu(two, cot_all, w_gate, w_up, w_down, collective_id):
    n_seq = lax.axis_size("seq")
    rows, width = two.shape
    units = w_gate.shape[1]
    tokens = 4 * rows
    shape = jax.ShapeDtypeStruct
    half = shape((2, tokens, width // 2), BF16)
    pair = shape((2, tokens, units), BF16)
    remote_count = 6 + n_seq + 9
    return pl.pallas_call(
        functools.partial(glu_kernel, n_seq),
        out_shape=(half, half, pair, pair, pair),
        in_specs=[VMEM] + [ANY] * 4,
        out_specs=(ANY,) * 5,
        scratch_shapes=[
            pltpu.VMEM((width, 2 * units), BF16),
            pltpu.VMEM((units, width), BF16),
            pltpu.VMEM((tokens, width), BF16),
            pltpu.VMEM((tokens, width), BF16),
            pltpu.VMEM((tokens, units), F32),
            pltpu.VMEM((2 * rows, 2 * units), F32),
            pltpu.VMEM((tokens, units), BF16),
            pltpu.VMEM((tokens, units), BF16),
            pltpu.VMEM((tokens, units), BF16),
            pltpu.SemaphoreType.DMA((remote_count,)),
            pltpu.SemaphoreType.DMA((remote_count,)),
            pltpu.SemaphoreType.DMA((4 + n_seq + 9,)),
        ],
        compiler_params=params(collective_id),
        name="glu",
    )(two, cot_all, w_gate, w_up, w_down)


class ZLine:
    def __init__(self, part, buf, sems, n_seq, width, lag, ahead, store=None, leave=None):
        self.part, self.buf, self.width, self.lag, self.ahead = part, buf, width, lag, ahead
        self.send_up, self.recv_up, self.send_down, self.recv_down = sems[:4]
        self.store, self.leave = store, leave
        self.s, self.f = lax.axis_index("seq"), lax.axis_index("fsdp")
        self.n_seq, self.nz = n_seq, n_seq // 2
        self.z = self.s // 2
        self.block = part.shape[0] // self.nz
        self.chunks = part.shape[1] // width
        self.steps = (self.nz - 1) * self.chunks
        self.calls = self.steps + lag * (self.nz - 2)

    def rows(self, t):
        return pl.ds(pl.multiple_of(t * self.block, self.block), self.block)

    def move(self, up, k, j):
        t = self.nz - 1 - k if up else k
        landing = t + 1 if up else t
        cols = tile(j, self.width)
        slot = k * self.chunks + j
        peer = lax.rem(self.s + (2 if up else self.n_seq - 2), self.n_seq)
        send, recv = (
            (self.send_up, self.recv_up) if up else (self.send_down, self.recv_down)
        )
        return remote(
            self.part.at[self.rows(t), cols],
            self.buf.at[self.rows(landing), cols],
            send.at[slot],
            recv.at[slot],
            (peer, self.f),
        )

    def feed(self, q):
        inside = q < self.steps
        q = jnp.minimum(q, self.steps - 1)
        k = q // self.chunks
        j = q - k * self.chunks

        @pl.when(inside & (self.z == 0))
        def _():
            self.move(True, k, j).start()

        @pl.when(inside & (self.z == self.nz - 1))
        def _():
            self.move(False, k, j).start()

    def nth(self, i):
        return jnp.where(self.z < self.nz // 2, self.nz - 1 - i, i)

    def load(self, local, src):
        order = [self.rows(self.nth(i)) for i in range(self.nz)]
        return [local.start(src.at[at], self.part.at[at]) for at in order]

    def feed_first(self):
        def step(q, _):
            self.feed(q)
            return 0

        lax.fori_loop(0, self.ahead, step, 0)

    def serve_one(self, up, q):
        z, nz = self.z, self.nz
        hops = z if up else nz - 1 - z
        q = q - self.lag * (hops - 1)
        inside = (hops >= 1) & (q >= 0) & (q < self.steps)
        q = jnp.clip(q, 0, self.steps - 1)
        k = q // self.chunks
        j = q - k * self.chunks
        left = nz - 1 - k - hops
        cols = tile(j, self.width)

        @pl.when(inside & (left >= 0))
        def _():
            self.move(up, k, j).wait_recv()

        @pl.when(inside & (left > 0))
        def _():
            t = nz - 1 - k if up else k
            landing = t + 1 if up else t
            own = self.part[self.rows(t), cols].astype(F32)
            came = self.buf[self.rows(landing), cols].astype(F32)
            self.part[self.rows(t), cols] = (own + came).astype(BF16)
            self.move(up, k, j).start()

    def serve(self, q, done=False):
        self.serve_one(True, q)
        self.serve_one(False, q)
        if done:
            j = q - (self.nz - 2) * self.chunks

            @pl.when((j >= 0) & (j < self.chunks))
            def _():
                self.finish(j)

    def serve_range(self, first, last, done=False):
        def step(q, _):
            self.feed(q + self.ahead)
            self.serve(q, done)
            return 0

        lax.fori_loop(first, last, step, 0)

    def finish(self, j):
        cols = tile(j, self.width)
        above = self.buf[self.rows(self.z), cols].astype(F32)
        below = self.buf[self.rows(self.z + 1), cols].astype(F32)
        own = self.part[self.rows(self.z), cols].astype(F32)
        own = own + jnp.where(self.z < self.nz - 1, above, 0.0)
        self.store(j, own + jnp.where(self.z > 0, below, 0.0))
        self.leave(j, True)

    def drain(self):
        for k in range(self.nz - 1):
            for up in (True, False):
                hops = self.z if up else self.nz - 1 - self.z

                @pl.when(hops < self.nz - 1 - k)
                def _():
                    def step(j, _):
                        self.move(up, k, j).wait_send()
                        return 0

                    lax.fori_loop(0, self.chunks, step, 0)

        def left(j, _):
            self.leave(j, False)
            return 0

        lax.fori_loop(0, self.chunks, left, 0)


def start_or_wait(copy, start):
    if start:
        copy.start()
    else:
        copy.wait()


def line_sems(n_seq, columns, width):
    count = (n_seq // 2 - 1) * (columns // width)
    leave = pltpu.SemaphoreType.DMA((columns // width,))
    return [pltpu.SemaphoreType.DMA((count,)) for _ in range(4)] + [leave]


def z_peers(n_seq):
    s = lax.axis_index("seq")
    f = lax.axis_index("fsdp")
    return [(lax.rem(s + 2 * k, n_seq), f) for k in range(1, n_seq // 2)]


def mm_tokens(left, right):
    return lax.dot_general(left, right, (((0,), (0,)), ((), ())), preferred_element_type=F32)


def down_kernel(
    n_seq,
    cot_half,
    act_pair,
    two_half,
    gate_pair,
    up_pair,
    w_gate,
    w_up,
    d_two,
    pair_part,
    down_out,
    cot_ref,
    act_ref,
    two_ref,
    gate_ref,
    up_ref,
    wg,
    wu,
    part,
    buf,
    rows_part,
    from_x,
    from_y,
    pass_x,
    pass_y,
    pair_ref,
    down_ref,
    send,
    recv,
    local_sems,
    *line,
):
    rows, width = d_two.shape
    units = act_pair.shape[1]
    s, f, fx, fy, fd = plane()
    links, local = Links(send, recv), Locals(local_sems)
    moves = (
        (cot_half, cot_ref),
        (act_pair, act_ref),
        (w_gate, wg),
        (w_up, wu),
        (gate_pair, gate_ref),
        (up_pair, up_ref),
        (two_half, two_ref),
    )
    loads = [local.start(src, dst) for src, dst in moves]
    enter([(s, fx), (s, fy)] + z_peers(n_seq))

    def store(j, value):
        down_ref[tile(j, 128)] = value.T

    def leave(j, start):
        at = tile(j, 128)
        copy = pltpu.make_async_copy(down_ref.at[at], down_out.at[at], line[4].at[j])
        start_or_wait(copy, start)

    z_sum = ZLine(part, buf, line, n_seq, 128, 3, 11, store, leave)
    block = z_sum.block
    loads[0].wait()
    loads[1].wait()

    def down_tile(i, _):
        t = z_sum.nth(i)
        part[z_sum.rows(t)] = mm_tokens(cot_ref[:, tile(t, block)], act_ref[...]).astype(BF16)
        return 0

    down_tile(jnp.int32(0), 0)
    z_sum.feed_first()
    lax.fori_loop(1, z_sum.nz, down_tile, 0)
    for copy in loads[2:]:
        copy.wait()

    def two_part(first, slots, base):
        at = slice(first * rows, (first + slots) * rows)

        def tile_of(n, _):
            cols = tile(n, 512)
            total = mm_t(gate_ref[at], wg[cols]) + mm_t(up_ref[at], wu[cols])
            rows_part[at, cols] = total.astype(BF16)
            z_sum.feed(base + n + z_sum.ahead)
            z_sum.serve(base + n)
            return 0

        lax.fori_loop(0, width // 512, tile_of, 0)

    count = width // 512
    two_part(3, 1, 0)
    far = reduce_start_far(links, rows_part, from_x, from_y, rows, s, fx, fy)
    two_part(1, 2, count)
    near = reduce_start_near(links, rows_part, from_x, from_y, rows, s, fx, fy)
    two_part(0, 1, 2 * count)
    served = 3 * count

    def pair_tiles(right, first, base):
        def tile_of(t, _):
            pair_ref[z_sum.rows(t), pl.ds(first, units)] = mm_tokens(
                two_ref[:, tile(t, block)], right[...]
            ).astype(BF16)
            z_sum.serve_range(base + 2 * t, base + 2 * t + 2, True)
            return 0

        lax.fori_loop(0, z_sum.nz, tile_of, 0)

    pair_tiles(gate_ref, 0, served)
    served += 2 * z_sum.nz
    passed = reduce_pass(links, far, rows_part, from_x, from_y, pass_x, pass_y, rows, s, fx, fy)
    pair_tiles(up_ref, units, served)
    served += 2 * z_sum.nz
    stay = local.start(pair_ref, pair_part)
    for copy in near + passed:
        copy.wait_recv()
    half = rows // 2
    d_two[:half] = rows_part[:half].astype(F32) + from_x[1].astype(F32) + from_y[2].astype(F32)
    d_two[half:] = rows_part[half:rows].astype(F32) + from_y[1].astype(F32) + from_x[2].astype(F32)
    z_sum.serve_range(served, z_sum.calls, True)
    z_sum.drain()
    sends_done(far, near, passed)
    stay.wait()


def down_sum(cot_half, act_pair, two_half, gate_pair, up_pair, w_gate, w_up, collective_id):
    n_seq = lax.axis_size("seq")
    tokens, units = act_pair.shape
    width = w_gate.shape[0]
    rows = tokens // 8
    half = (rows // 2, width)
    own = cot_half.shape[1]
    block = width // n_seq
    shape = jax.ShapeDtypeStruct
    return pl.pallas_call(
        functools.partial(down_kernel, n_seq),
        out_shape=(
            shape((rows, width), F32),
            shape((own, 2 * units), BF16),
            shape((units, block), F32),
        ),
        in_specs=[ANY] * 7,
        out_specs=(VMEM, ANY, ANY),
        scratch_shapes=[
            pltpu.VMEM((tokens, own), BF16),
            pltpu.VMEM((tokens, units), BF16),
            pltpu.VMEM((tokens, own), BF16),
            pltpu.VMEM((tokens, units), BF16),
            pltpu.VMEM((tokens, units), BF16),
            pltpu.VMEM((width, units), BF16),
            pltpu.VMEM((width, units), BF16),
            pltpu.VMEM((own, units), BF16),
            pltpu.VMEM((own + block, units), BF16),
            pltpu.VMEM((tokens // 2, width), BF16),
            pltpu.VMEM((3,) + half, BF16),
            pltpu.VMEM((3,) + half, BF16),
            pltpu.VMEM(half, BF16),
            pltpu.VMEM(half, BF16),
            pltpu.VMEM((own, 2 * units), BF16),
            pltpu.VMEM((units, block), F32),
            pltpu.SemaphoreType.DMA((6,)),
            pltpu.SemaphoreType.DMA((6,)),
            pltpu.SemaphoreType.DMA((8,)),
        ]
        + line_sems(n_seq, units, 128),
        compiler_params=params(collective_id),
        name="down_sum",
    )(cot_half, act_pair, two_half, gate_pair, up_pair, w_gate, w_up)


def pair_kernel(
    n_seq,
    lengths,
    hidden,
    cot,
    glu_gain,
    gate_gain,
    table,
    scale_g,
    d_two,
    middle,
    pair_part,
    w_out,
    w_in,
    w_fg,
    w_gt,
    gate_raw,
    state_b,
    out_raw,
    in_raw,
    fg_raw,
    before_in,
    normed_half,
    pair_grad,
    mixer_part,
    d_normed_out,
    d_middle_out,
    d_glu_gain,
    d_gain,
    d_bounds,
    d_normed,
    d_middle,
    pair_ref,
    part,
    buf,
    wo,
    wv,
    mixed_all,
    mixed_mate,
    normed_ref,
    d_proj,
    out_gate,
    gate_ref,
    state_ref,
    raw_ref,
    in_ref,
    fg_ref,
    before,
    p_ref,
    q_ref,
    stage,
    rows_part,
    from_x,
    from_y,
    pass_x,
    pass_y,
    dots,
    keep_ref,
    end_p,
    end_s,
    carr,
    total,
    gathered,
    send,
    recv,
    exchange_send,
    exchange_recv,
    local_sems,
    tile_sems,
    *line,
):
    rows, width = hidden.shape
    chans = w_in.shape[1]
    tokens = 4 * rows
    lanes_of = [slice(c, c + 128) for c in range(0, chans, 128)]
    count = len(lanes_of)
    blocks = 4 * count
    step_len = rows // 8
    s, f, fx, fy, fd = plane()
    groups = [f, fx, fy, fd]
    core = s % 2
    mate = (s + 1 - 2 * core, f)
    links, local = Links(send, recv), Locals(local_sems)

    def store(j, value):
        pair_ref[:, tile(j, 256)] = value

    def leave(j, start):
        at = tile(j, 256)
        copy = pltpu.make_async_copy(pair_ref.at[:, at], pair_grad.at[:, at], line[4].at[j])
        start_or_wait(copy, start)

    z_sum = ZLine(part, buf, line, n_seq, 256, 2, 11, store, leave)
    blocks_in = z_sum.load(local, pair_part)
    rows_in = [local.start(d_two, d_middle), local.start(middle, d_normed)]
    loads = [local.start(w_out, wo)]
    loads += [
        local.start(src, dst)
        for src, dst in (
            (gate_raw, gate_ref),
            (state_b, state_ref),
            (out_raw, raw_ref),
            (in_raw, in_ref),
            (fg_raw, fg_ref),
            (before_in, before),
        )
    ]
    weights = [
        local.start(w, wv.at[:, pl.ds(i * chans, chans)]) for i, w in enumerate((w_in, w_fg, w_gt))
    ]
    weights.append(local.start(normed_half, normed_ref))
    enter([(s, fx), (s, fy), (s, fd)] + seq_peers(n_seq))
    blocks_in[0].wait()
    z_sum.feed_first()
    served = 0

    def serve(number):
        nonlocal served
        z_sum.serve_range(served, served + number)
        served += number

    d_glu_gain[...] = jnp.zeros_like(d_glu_gain)
    wait_all(rows_in, blocks_in[1:])

    def middle_rows(i, _):
        at = pl.ds(pl.multiple_of(i * 16, 16), 16)
        value, came = d_normed[at], d_middle[at]
        scale = lax.rsqrt(jnp.mean(value * value, -1, keepdims=True) + epsilon)
        scaled = glu_gain[...] * came
        mean = jnp.mean(scaled * value, -1, keepdims=True)
        grad = cot[at].astype(F32) + scale * scaled - value * (scale**3 * mean)
        d_middle[at] = grad
        grad_b = grad.astype(BF16)
        mixed_all[at] = grad_b
        own_dot = jnp.sum(
            grad_b.astype(F32) * (value - hidden[at].astype(F32)), -1, keepdims=True
        )
        dots[0, at] = jnp.broadcast_to(own_dot, (16, 128))
        d_glu_gain[...] += jnp.sum(came * value * scale, 0, keepdims=True)
        return 0

    lax.fori_loop(0, rows // 16, middle_rows, 0)
    outs = [local.start(d_middle, d_middle_out)]
    own = gather_start(links, mixed_all, mixed_all, rows, s, fx, fy)
    dot_copies = [
        links.start(dots.at[0], dots.at[k], (s, peer)) for k, peer in ((1, fx), (2, fy), (3, fd))
    ]
    bound = bounds_slice(table, f * chans, chans)
    for k in range(4):
        keep_ref[k] = keep_rows(lengths, groups[k], s * rows, rows)
    d_gain[...] = jnp.zeros_like(d_gain)
    serve(1)
    for copy in loads:
        copy.wait()

    def out_rows(first, slots):
        stage[: slots * rows] = mm_t(mixed_all[first * rows : (first + slots) * rows], wo[...])
        for i in range(slots):
            k = first + i
            scale = scale_g[k]
            for c, lanes in enumerate(lanes_of):
                n = k * count + c
                gain = gate_gain[:, pl.ds(pl.multiple_of(f * chans + c * 128, 128), 128)]
                d_out = stage[i * rows : (i + 1) * rows, lanes]
                gate = gate_ref[k, :, lanes]
                sigma = jax.nn.sigmoid(gate)
                silu = gate * sigma
                state = state_ref[k, :, lanes].astype(F32)
                weighed = d_out * (state * scale)
                d_gain[:, lanes] += jnp.sum(weighed * silu, 0, keepdims=True)
                at = slice(k * rows, (k + 1) * rows)
                d_proj[at, 2 * chans + c * 128 : 2 * chans + (c + 1) * 128] = (
                    weighed * gain * silu_slope(gate, sigma)
                ).astype(BF16)
                out_gate[at, lanes] = (raw_ref[at, lanes].astype(F32) * scale).astype(BF16)
                d_state = scale * (d_out * gain * silu) - state * (
                    scale * scale * (dots[k] / width)
                )
                q_ref[n] = d_state.astype(BF16).astype(F32)
                edge = bound[:, lanes]
                forget = edge + (1.0 - edge) * jax.nn.sigmoid(fg_ref[k, :, lanes].astype(F32))
                p_ref[n] = forget * keep_ref[k]

    out_rows(0, 1)
    later = gather_forward(links, own, mixed_all, rows, s, fx, fy)
    serve(2)
    gather_middle(own)
    for copy in dot_copies:
        copy.wait_recv()
    out_rows(1, 2)
    serve(3)
    gather_far(later)
    out_rows(3, 1)
    serve(2)
    own_rows, mate_rows = pl.ds(0, tokens), pl.ds(tokens, tokens)
    last = pl.ds(2 * chans, chans)
    swaps = [
        links.start(out_gate.at[own_rows], out_gate.at[mate_rows], mate),
        links.start(d_proj.at[own_rows, last], d_proj.at[mate_rows, last], mate),
    ]
    wide = z_sum.block
    for t in range(n_seq // 2):
        theirs = pl.ds(pl.multiple_of((2 * t + 1 - core) * wide, wide), wide)
        swaps.append(
            links.start(mixed_all.at[:, theirs], mixed_mate.at[:, pl.ds(t * wide, wide)], mate)
        )

    def scan_step(i, carry):
        new = []
        at = pl.ds(step_len - 1 - i, 8, stride=step_len)
        for n, (product, message) in enumerate(carry):
            a = p_ref[n, at, :]
            acc = q_ref[n, at, :] + message
            p_ref[n, at, :] = product
            q_ref[n, at, :] = acc
            new.append((product * a, a * acc))
        return tuple(new)

    start = tuple((jnp.ones((8, 128), F32), jnp.zeros((8, 128), F32)) for _ in range(blocks))
    ends = lax.fori_loop(0, step_len, scan_step, start)
    for n, (product, message) in enumerate(ends):
        end_p[8 * n : 8 * n + 8] = product
        end_s[8 * n : 8 * n + 8] = message
    p_all, s_all = segment_totals(end_p, end_s, blocks, range(7, -1, -1))
    total[:blocks] = p_all
    total[blocks:] = s_all
    copies = start_exchange(total, gathered, exchange_send, exchange_recv, n_seq)
    serve(2)
    wait_all(copies)
    carry = jnp.zeros((blocks, 128), F32)
    for j in range(n_seq - 1, 0, -1):
        carry = jnp.where(j > s, gathered[j, blocks:] + gathered[j, :blocks] * carry, carry)
    spread_carry(carry, carr, end_p, end_s, blocks, range(7, -1, -1))

    def finish(n, _):
        enter_state = carr[pl.ds(pl.multiple_of(n * 8, 8), 8)]
        for i in range(step_len):
            at = pl.ds(i, 8, stride=step_len)
            q_ref[n, at, :] = q_ref[n, at, :] + p_ref[n, at, :] * enter_state
        return 0

    lax.fori_loop(0, blocks, finish, 0)
    d_bounds[...] = jnp.zeros_like(d_bounds)
    for k in range(4):
        at = slice(k * rows, (k + 1) * rows)
        for c, lanes in enumerate(lanes_of):
            acc = q_ref[k * count + c]
            edge = bound[:, lanes]
            sigma_f = jax.nn.sigmoid(fg_ref[k, :, lanes].astype(F32))
            forget = edge + (1.0 - edge) * sigma_f
            value = in_ref[k, :, lanes].astype(F32)
            sigma_i = jax.nn.sigmoid(value)
            d_forget = acc * (before[k * count + c] * keep_ref[k] - value * sigma_i)
            d_proj[at, lanes] = (acc * (1.0 - forget) * silu_slope(value, sigma_i)).astype(BF16)
            d_sigma = d_forget * (1.0 - sigma_f)
            d_proj[at, chans + c * 128 : chans + (c + 1) * 128] = (
                d_sigma * (1.0 - edge) * sigma_f
            ).astype(BF16)
            d_bounds[:, lanes] += jnp.sum(d_sigma, 0, keepdims=True)
    first = pl.ds(0, 2 * chans)
    swaps.append(links.start(d_proj.at[own_rows, first], d_proj.at[mate_rows, first], mate))
    serve(2)
    for copy in weights:
        copy.wait()

    def normed_part(first_slot, slots):
        at = slice(first_slot * rows, (first_slot + slots) * rows)

        def tile_of(n, _):
            cols = tile(n, 512)
            rows_part[at, cols] = mm_t(d_proj[at], wv[cols]).astype(BF16)
            return 0

        lax.fori_loop(0, width // 512, tile_of, 0)

    normed_part(3, 1)
    far = reduce_start_far(links, rows_part, from_x, from_y, rows, s, fx, fy)
    normed_part(1, 2)
    near = reduce_start_near(links, rows_part, from_x, from_y, rows, s, fx, fy)
    normed_part(0, 1)
    serve(3)
    for copy in swaps:
        copy.wait_recv()

    def tile_out(t):
        slot = lax.rem(t, 2)
        return pltpu.make_async_copy(
            wo.at[tile(slot, wide)], mixer_part.at[z_sum.rows(t)], tile_sems.at[slot]
        )

    def mixer_tile(t, _):
        @pl.when(t >= 2)
        def _():
            tile_out(t - 2).wait()

        at = tile(lax.rem(t, 2), wide)
        ours = mixed_all[:, tile(2 * t + core, wide)]
        out_part = mm_tokens(ours, out_gate[:tokens])
        out_part = out_part + mm_tokens(mixed_mate[:, tile(t, wide)], out_gate[tokens:])
        wo[at, :chans] = out_part.astype(BF16)
        wo[at, chans:] = mm_tokens(normed_ref[:, tile(t, wide)], d_proj[...]).astype(BF16)
        tile_out(t).start()
        return 0

    lax.fori_loop(0, 1, mixer_tile, 0)
    passed = reduce_pass(links, far, rows_part, from_x, from_y, pass_x, pass_y, rows, s, fx, fy)
    serve(1)
    lax.fori_loop(1, z_sum.nz, mixer_tile, 0)
    serve(2)
    for copy in near + passed:
        copy.wait_recv()
    half = rows // 2
    d_normed[:half] = rows_part[:half].astype(F32) + from_x[1].astype(F32) + from_y[2].astype(F32)
    d_normed[half:] = (
        rows_part[half:rows].astype(F32) + from_y[1].astype(F32) + from_x[2].astype(F32)
    )
    outs.append(local.start(d_normed, d_normed_out))
    z_sum.serve_range(served, z_sum.calls, True)
    z_sum.drain()
    sends_done(own, later, dot_copies, swaps, far, near, passed)
    for t in range(z_sum.nz - 2, z_sum.nz):
        tile_out(jnp.int32(t)).wait()
    wait_all(outs)


def pair_sum(
    lengths, own_rows, gains, table, scale_g, float_rows, pair_part, weights, saved, normed_half, cid
):
    n_seq = lax.axis_size("seq")
    rows, width = own_rows[0].shape
    chans = weights[1].shape[1]
    own, columns = pair_part.shape
    tokens = 4 * rows
    blocks = 4 * chans // 128
    block = width // n_seq
    half = (rows // 2, width)
    shape = jax.ShapeDtypeStruct
    exchange = pltpu.SemaphoreType.DMA((n_seq,))
    count = 18 + n_seq // 2
    return pl.pallas_call(
        functools.partial(pair_kernel, n_seq),
        out_shape=(
            shape((block, columns), F32),
            shape((own, 4 * chans), BF16),
            shape((rows, width), F32),
            shape((rows, width), F32),
            shape((1, width), F32),
            shape((1, chans), F32),
            shape((1, chans), F32),
        ),
        in_specs=[pl.BlockSpec(memory_space=pltpu.SMEM)] + [VMEM] * 6 + [ANY] * 14,
        out_specs=(ANY,) * 4 + (VMEM,) * 3,
        scratch_shapes=[
            pltpu.VMEM((rows, width), F32),
            pltpu.VMEM((rows, width), F32),
            pltpu.VMEM((block, columns), F32),
            pltpu.VMEM((own, columns), BF16),
            pltpu.VMEM((own + block, columns), BF16),
            pltpu.VMEM((chans, width), BF16),
            pltpu.VMEM((width, 3 * chans), BF16),
            pltpu.VMEM((tokens, width), BF16),
            pltpu.VMEM((tokens, width // 2), BF16),
            pltpu.VMEM((2 * tokens, width // 2), BF16),
            pltpu.VMEM((2 * tokens, 3 * chans), BF16),
            pltpu.VMEM((2 * tokens, chans), BF16),
            pltpu.VMEM((4, rows, chans), F32),
            pltpu.VMEM((4, rows, chans), BF16),
            pltpu.VMEM((tokens, chans), BF16),
            pltpu.VMEM((4, rows, chans), BF16),
            pltpu.VMEM((4, rows, chans), BF16),
            pltpu.VMEM((blocks, rows, 128), F32),
            pltpu.VMEM((blocks, rows, 128), F32),
            pltpu.VMEM((blocks, rows, 128), F32),
            pltpu.VMEM((2 * rows, chans), F32),
            pltpu.VMEM((tokens, width), BF16),
            pltpu.VMEM((3,) + half, BF16),
            pltpu.VMEM((3,) + half, BF16),
            pltpu.VMEM(half, BF16),
            pltpu.VMEM(half, BF16),
            pltpu.VMEM((4, rows, 128), F32),
            pltpu.VMEM((4, rows, 128), F32),
            pltpu.VMEM((8 * blocks, 128), F32),
            pltpu.VMEM((8 * blocks, 128), F32),
            pltpu.VMEM((8 * blocks, 128), F32),
            pltpu.VMEM((2 * blocks, 128), F32),
            pltpu.VMEM((n_seq, 2 * blocks, 128), F32),
            pltpu.SemaphoreType.DMA((count,)),
            pltpu.SemaphoreType.DMA((count,)),
            exchange,
            exchange,
            pltpu.SemaphoreType.DMA((15 + n_seq // 2,)),
            pltpu.SemaphoreType.DMA((2,)),
        ]
        + line_sems(n_seq, columns, 256),
        compiler_params=params(cid),
        name="pair_sum",
    )(
        lengths,
        *own_rows,
        *gains,
        table,
        scale_g,
        *float_rows,
        pair_part,
        *weights,
        *saved,
        normed_half,
    )


def final_kernel(
    n_seq,
    n_fsdp,
    d_normed,
    d_middle,
    hidden,
    middle,
    norm_gain,
    d_glu_gain,
    d_gain,
    d_bounds,
    table,
    mixer_part,
    act_pair,
    w_down,
    output,
    d_hidden,
    out_grad,
    rest_grad,
    sums,
    d_table,
    out_ref,
    rest_ref,
    part,
    buf,
    act,
    wd,
    rows_part,
    from_x,
    from_y,
    pass_x,
    pass_y,
    norm_sum,
    terms,
    quarters_in,
    terms_q,
    over_seq,
    along_sum,
    over_fsdp,
    send,
    recv,
    local_sems,
    *line,
):
    rows, width = middle.shape
    chans = d_gain.shape[1]
    tokens = 4 * rows
    s, f, fx, fy, fd = plane()
    links, local = Links(send, recv), Locals(local_sems)
    head = chans // 256

    def store(j, value):
        @pl.when(j < head)
        def _():
            out_ref[tile(j, 256)] = value.T

        @pl.when(j >= head)
        def _():
            rest_ref[:, tile(j - head, 256)] = value

    def leave(j, start):
        @pl.when(j < head)
        def _():
            at = tile(j, 256)
            copy = pltpu.make_async_copy(out_ref.at[at], out_grad.at[at], line[4].at[j])
            start_or_wait(copy, start)

        @pl.when(j >= head)
        def _():
            at = tile(j - head, 256)
            copy = pltpu.make_async_copy(rest_ref.at[:, at], rest_grad.at[:, at], line[4].at[j])
            start_or_wait(copy, start)

    z_sum = ZLine(part, buf, line, n_seq, 256, 2, 8, store, leave)
    blocks_in = z_sum.load(local, mixer_part)
    loads = [
        local.start(act_pair.at[pl.ds(0, tokens)], act),
        local.start(w_down, wd),
    ]
    along = seq_peers(n_seq)
    across = [(s, fx), (s, fy), (s, fd)]
    enter(across + along)
    blocks_in[0].wait()
    z_sum.feed_first()
    served = 0

    def serve(number):
        nonlocal served
        z_sum.serve_range(served, served + number)
        served += number

    norm_sum[...] = jnp.zeros_like(norm_sum)

    def hidden_rows(i, _):
        at = pl.ds(pl.multiple_of(i * 16, 16), 16)
        value, came = hidden[at].astype(F32), d_normed[at]
        scale = lax.rsqrt(jnp.mean(value * value, -1, keepdims=True) + epsilon)
        scaled = norm_gain[...] * came
        mean = jnp.mean(scaled * value, -1, keepdims=True)
        d_hidden[at] = (d_middle[at] + scale * scaled - value * (scale**3 * mean)).astype(BF16)
        norm_sum[...] += jnp.sum(came * value * scale, 0, keepdims=True)
        return 0

    wait_all(blocks_in[1:], loads)

    def glu_part(first, slots):
        at = slice(first * rows, (first + slots) * rows)

        def tile_of(n, _):
            cols = tile(n, 512)
            rows_part[at, cols] = mm(act[at], wd[:, cols]).astype(BF16)
            return 0

        lax.fori_loop(0, width // 512, tile_of, 0)

    glu_part(3, 1)
    far = reduce_start_far(links, rows_part, from_x, from_y, rows, s, fx, fy)
    glu_part(1, 2)
    near = reduce_start_near(links, rows_part, from_x, from_y, rows, s, fx, fy)
    glu_part(0, 1)
    serve(2)
    lax.fori_loop(0, rows // 16, hidden_rows, 0)
    terms[...] = jnp.zeros_like(terms)
    for q in range(4):
        terms[q, 0:1] = norm_sum[:, q * chans : (q + 1) * chans]
        terms[q, 1:2] = d_glu_gain[:, q * chans : (q + 1) * chans]
    quarter_copies = [
        links.start(terms.at[peer], quarters_in.at[k], (s, peer))
        for k, peer in enumerate((fx, fy, fd))
    ]
    serve(1)
    passed = reduce_pass(links, far, rows_part, from_x, from_y, pass_x, pass_y, rows, s, fx, fy)
    serve(2)
    quarter = terms[pl.ds(f, 1)][0]
    for k, copy in enumerate(quarter_copies):
        copy.wait_recv()
        quarter = quarter + quarters_in[k]
    half = chans // 2
    for first, cols in ((0, slice(0, half)), (4, slice(half, chans))):
        terms_q[first : first + 2] = quarter[:2, cols]
        terms_q[first + 2 : first + 3] = d_gain[:, cols]
        terms_q[first + 3 : first + 4] = d_bounds[:, cols]
    seq_copies = [links.start(terms_q, over_seq.at[k], peer) for k, peer in enumerate(along)]
    serve(1)
    total = terms_q[...]
    for k, copy in enumerate(seq_copies):
        copy.wait_recv()
        total = total + over_seq[k]
    along_sum[...] = total
    fsdp_copies = [links.start(along_sum, over_fsdp.at[k], peer) for k, peer in enumerate(across)]
    serve(2)
    for copy in near + passed:
        copy.wait_recv()
    middle_half = rows // 2
    for first, one, other in (
        (0, from_x.at[1], from_y.at[2]),
        (middle_half, from_y.at[1], from_x.at[2]),
    ):
        at = slice(first, first + middle_half)
        added = rows_part[at].astype(F32) + one[...].astype(F32) + other[...].astype(F32)
        output[at] = (middle[at] + added).astype(BF16)
    serve(1)
    for copy in fsdp_copies:
        copy.wait_recv()
    for k, group in enumerate((f, fx, fy, fd)):
        total = along_sum[...] if k == 0 else over_fsdp[k - 1]
        for i in range(2):
            at = pl.ds(pl.multiple_of(group * chans + i * half, 128), half)
            sums[:, at] = total[4 * i : 4 * i + 4]
    powers = jnp.exp(table[...] - jnp.max(table[...], 0, keepdims=True))
    soft = powers / jnp.sum(powers, 0, keepdims=True)
    row = lax.broadcasted_iota(jnp.int32, soft.shape, 0)
    chosen = jnp.where((row >= 1) & (row <= LAYER), 1.0, 0.0)
    bound = jnp.sum(soft * chosen, 0, keepdims=True)
    d_table[...] = soft * (chosen - bound) * sums[3:4]
    z_sum.serve_range(served, z_sum.calls, True)
    z_sum.drain()
    sends_done(far, near, passed, quarter_copies, seq_copies, fsdp_copies)


def final_sum(rows_in, gains, table, mixer_part, act_pair, w_down, cid):
    n_seq, n_fsdp = lax.axis_size("seq"), lax.axis_size("fsdp")
    rows, width = rows_in[0].shape
    own, columns = mixer_part.shape
    units = w_down.shape[0]
    chans = columns // 4
    tokens = 4 * rows
    block = width // n_seq
    half = (rows // 2, width)
    terms = (8, chans // 2)
    shape = jax.ShapeDtypeStruct
    count = 6 + n_seq - 1 + 2 * (n_fsdp - 1)
    return pl.pallas_call(
        functools.partial(final_kernel, n_seq, n_fsdp),
        out_shape=(
            shape((rows, width), BF16),
            shape((rows, width), BF16),
            shape((chans, block), F32),
            shape((block, 3 * chans), F32),
            shape((4, width), F32),
            shape(table.shape, F32),
        ),
        in_specs=[VMEM] * 9 + [ANY] * 3,
        out_specs=(VMEM, VMEM, ANY, ANY, VMEM, VMEM),
        scratch_shapes=[
            pltpu.VMEM((chans, block), F32),
            pltpu.VMEM((block, 3 * chans), F32),
            pltpu.VMEM((own, columns), BF16),
            pltpu.VMEM((own + block, columns), BF16),
            pltpu.VMEM((tokens, units), BF16),
            pltpu.VMEM((units, width), BF16),
            pltpu.VMEM((tokens, width), BF16),
            pltpu.VMEM((3,) + half, BF16),
            pltpu.VMEM((3,) + half, BF16),
            pltpu.VMEM(half, BF16),
            pltpu.VMEM(half, BF16),
            pltpu.VMEM((1, width), F32),
            pltpu.VMEM((n_fsdp, 8, chans), F32),
            pltpu.VMEM((n_fsdp - 1, 8, chans), F32),
            pltpu.VMEM(terms, F32),
            pltpu.VMEM((n_seq - 1,) + terms, F32),
            pltpu.VMEM(terms, F32),
            pltpu.VMEM((n_fsdp - 1,) + terms, F32),
            pltpu.SemaphoreType.DMA((count,)),
            pltpu.SemaphoreType.DMA((count,)),
            pltpu.SemaphoreType.DMA((2 + n_seq // 2,)),
        ]
        + line_sems(n_seq, columns, 256),
        compiler_params=params(cid),
        name="final_sum",
    )(*rows_in, *gains, table, mixer_part, act_pair, w_down)


def hand_over_kernel(count, pieces, *refs):
    sources, targets = refs[: len(refs) - 2 * count - 2], refs[len(refs) - 2 * count - 2 :]
    kept, arrived, left = targets[count : 2 * count], targets[2 * count], targets[2 * count + 1]
    loads, stores = [], []
    for n, (i, source, first, rows, column) in enumerate(pieces):
        at = pl.ds(first, rows)
        src = sources[source].at[at, pl.ds(column, kept[i].shape[1])]
        loads.append(copy_in(src, kept[i].at[at], arrived.at[n]))
    for n, (i, source, first, rows, column) in enumerate(pieces):
        at = pl.ds(first, rows)
        loads[n].wait()
        stores.append(copy_in(kept[i].at[at], targets[i].at[at], left.at[n]))
    for store in stores:
        store.wait()


def hand_over(arrays, wanted):
    pieces, shapes = [], []
    for i, (source, column, columns) in enumerate(wanted):
        x = arrays[source]
        height = x.shape[0]
        parts = max(1, height * columns * x.dtype.itemsize >> 18)
        parts = parts if height % (parts * 16) == 0 else 1
        rows = height // parts
        pieces += [(i, source, n * rows, rows, column) for n in range(parts)]
        shapes.append(((height, columns), x.dtype))
    return pl.pallas_call(
        functools.partial(hand_over_kernel, len(wanted), tuple(pieces)),
        out_shape=tuple(jax.ShapeDtypeStruct(*x) for x in shapes),
        in_specs=[ANY] * len(arrays),
        out_specs=(ANY,) * len(wanted),
        scratch_shapes=[pltpu.VMEM(*x) for x in shapes]
        + [pltpu.SemaphoreType.DMA((len(pieces),))] * 2,
        compiler_params=pltpu.CompilerParams(vmem_limit_bytes=56 << 20),
        name="hand_over",
    )(*arrays)


def plane_device(
    hidden,
    lengths,
    w_input,
    w_forget,
    w_gate_out,
    w_output,
    norm_gain,
    gate_gain,
    glu_gain,
    lower_table,
    w_glu_gate,
    w_glu_up,
    w_glu_down,
    cotangent,
):
    hidden, cotangent = hidden[0], cotangent[0]
    tokens = 4 * hidden.shape[0]
    gains = (norm_gain[None], gate_gain[None], glu_gain[None])
    (
        normed_half,
        cot_all,
        in_raw,
        fg_raw,
        gate_raw,
        state_b,
        out_raw,
        before,
        scale_g,
        middle,
        normed_two,
    ) = mixer_forward(
        lengths,
        hidden,
        cotangent,
        gains,
        lower_table,
        (w_input, w_forget, w_gate_out, w_output),
        0,
    )
    two_half, cot_half, act_pair, gate_pair, up_pair = glu(
        normed_two, cot_all, w_glu_gate, w_glu_up, w_glu_down, 1
    )
    d_normed_two, pair_part, down_grad = down_sum(
        *(x.reshape(2 * tokens, -1) for x in (cot_half, act_pair, two_half, gate_pair, up_pair)),
        w_glu_gate,
        w_glu_up,
        2,
    )
    pair_grad, mixer_part, d_normed, d_middle, d_glu_gain, d_gain, d_bounds = pair_sum(
        lengths,
        (hidden, cotangent),
        (gains[2], gains[1]),
        lower_table,
        scale_g,
        (d_normed_two, middle),
        pair_part,
        (w_output, w_input, w_forget, w_gate_out),
        (gate_raw, state_b, out_raw, in_raw, fg_raw, before),
        normed_half.reshape(2 * tokens, -1),
        3,
    )
    output, d_hidden, out_grad, rest_grad, sums, d_table = final_sum(
        (d_normed, d_middle, hidden, middle),
        (gains[0], d_glu_gain, d_gain, d_bounds),
        lower_table,
        mixer_part,
        act_pair.reshape(2 * tokens, -1),
        w_glu_down,
        4,
    )
    width, chans, units = hidden.shape[1], w_input.shape[1], w_glu_gate.shape[1]
    block = down_grad.shape[1]
    (
        down_grad,
        gate_grad,
        up_grad,
        output,
        d_hidden,
        d_table,
        out_grad,
        in_grad,
        fg_grad,
        gt_grad,
    ) = hand_over(
        (down_grad, pair_grad, output, d_hidden, d_table, out_grad, rest_grad),
        (
            (0, 0, block),
            (1, 0, units),
            (1, units, units),
            (2, 0, width),
            (3, 0, width),
            (4, 0, width),
            (5, 0, block),
            (6, 0, chans),
            (6, chans, chans),
            (6, 2 * chans, chans),
        ),
    )
    return (
        output[None],
        d_hidden[None],
        in_grad,
        fg_grad,
        gt_grad,
        out_grad,
        sums[0],
        sums[2],
        sums[1],
        d_table,
        gate_grad,
        up_grad,
        down_grad,
    )


def fits_plane(mesh):
    return mesh.shape["fsdp"] == 4 and mesh.shape["seq"] % 2 == 0


def solution(mesh):
    rows_spec = P("fsdp", "seq", None)
    columns = P(None, "fsdp")
    placed = (
        rows_spec,
        P(),
        columns,
        columns,
        columns,
        P("fsdp", None),
        P(),
        P(),
        P(),
        P(),
        columns,
        columns,
        P("fsdp", None),
        rows_spec,
    )
    by_rows, by_columns = P("seq", "fsdp"), P("fsdp", "seq")
    return jax.shard_map(
        plane_device if fits_plane(mesh) else per_device,
        mesh=mesh,
        in_specs=placed,
        out_specs=(
            rows_spec,
            rows_spec,
            by_rows,
            by_rows,
            by_rows,
            by_columns,
            P(),
            P(),
            P(),
            P(),
            by_rows,
            by_rows,
            by_columns,
        ),
        check_vma=False,
    )
```

profile of v0, /device:TPU:8, one launch (start us, length us, event | category | flops | bytes accessed | tf_op | source)
XLA Modules:
  0.0 361.0 jit_solution(11054592999861989171)
XLA Ops:
  0.6 76.3 %mixer_forward.1 = (bf16[2,640,1024]{2,1,0:T(8,128)(2,1)}, bf16[640,2048]{1,0:T(8,128)(2,1)}, bf16[4,160,512]{2,1,0:T(8,128)(2,1)}, bf16[4,160,512]{2,1,0:T(8,12...) custom-call(s32[4,4]{1,0:T(4,128)} %lengths.3, ...), custom_call_target="tpu_custom_call" | custom-call | tf_op jit(solution)/shard_map/mixer_forward/pallas_call | solution.py:928
  76.9 34.8 %glu.1 = (bf16[2,640,1024]{2,1,0:T(8,128)(2,1)}, bf16[2,640,1024]{2,1,0:T(8,128)(2,1)}, bf16[2,640,1408]{2,1,0:T(8,128)(2,1)}, bf16[2,640,1408]{2,1,0:T(8,128)(2,1)}, bf16[2,640,1408]{2,1,0:T(8,128)(2,1)}) custom-call(bf16[160,2048]{1,0:T(8,128)(2,1)} %get-tuple-element.55.two, bf16[640,2048]{1,0:T(8,128)(2,1)} %get-tuple-element.56.cot_all, ...), custom_call_target="tpu_custom_call" | custom-call | tf_op jit(solution)/shard_map/glu/pallas_call | solution.py:1107
  111.8 56.6 %down_sum.1 = (f32[160,2048]{1,0:T(8,128)}, bf16[1024,2816]{1,0:T(8,128)(2,1)}, f32[1408,256]{1,0:T(8,128)}) custom-call(bf16[1280,1024]{1,0:T(8,128)(2,1)} %bitcast.27, bf16[1280,1408]{1,0:T(8,128)(2,1)} %bitcast.16, bf16[1280,1024]{1,0:T(8,128)(2,1)} %bitcast.26, bf16[1280,1408]{1,0:T(8,128)(2,1)} %bitcast.21, bf16[1280,1408]{1,0:T(8,128)(2,1)} %bitcast.22, ...), custom_call_target="tpu_custom_call" | custom-call | tf_op jit(solution)/shard_map/down_sum/pallas_call | solution.py:1416
  168.3 106.6 %pair_sum.1 = (f32[256,2816]{1,0:T(8,128)}, bf16[1024,2048]{1,0:T(8,128)(2,1)}, f32[160,2048]{1,0:T(8,128)}, f32[160,2048]{1,0:T(8,128)}, f32[1,2048]{1,0:T(1,128)}, /*index=5*/f32[1,512]{1,0:T(1,128)}, f32[1,512]{1,0:T(1,128)}) custom-call(s32[4,4]{1,0:T(4,128)} %lengths.3, bf16[160,2048]{1,0:T(8,128)(2,1)} %bitcast.19, bf16[160,2048]{1,0:T(8,128)(2,1)} %bitcast.24, ...), custom_call_target="tpu_custom_call" | custom-call | tf_op jit(solution)/shard_map/pair_sum/pallas_call | solution.py:1791
  274.9 78.8 %final_sum.1 = (bf16[160,2048]{1,0:T(8,128)(2,1)}, bf16[160,2048]{1,0:T(8,128)(2,1)}, f32[512,256]{1,0:T(8,128)}, f32[256,1536]{1,0:T(8,128)}, f32[4,2048]{1,0:T(4,128)}, /*index=5*/f32[24,2048]{1,0:T(8,128)}) custom-call(f32[160,2048]{1,0:T(8,128)} %get-tuple-element.75.d_normed, f32[160,2048]{1,0:T(8,128)} %get-tuple-element.76.d_middle, ...), custom_call_target="tpu_custom_call" | custom-call | tf_op jit(solution)/shard_map/final_sum/pallas_call | solution.py:2054
  353.8 0.0 copy-start
  353.8 6.6 %hand_over.1 = (f32[1408,256]{1,0:T(8,128)}, f32[256,1408]{1,0:T(8,128)}, f32[256,1408]{1,0:T(8,128)}, bf16[160,2048]{1,0:T(8,128)(2,1)}, bf16[160,2048]{1,0:T(8...) custom-call(f32[1408,256]{1,0:T(8,128)} %get-tuple-element.62.refs_0, ...), custom_call_target="tpu_custom_call" | custom-call | tf_op jit(solution)/shard_map/hand_over/pallas_call | solution.py:2121
  360.4 0.0 copy-done
  360.4 0.6 fusion
Async XLA Ops:
  353.8 6.6 %copy-start = (f32[4,2048]{1,0:T(4,128)S(1)}, f32[4,2048]{1,0:T(4,128)}, u32[]{:S(2)}) copy-start(f32[4,2048]{1,0:T(4,128)} %get-tuple-element.92) | copy-start | bytes 98308
where the time goes:
time: 361 us
  Pallas kernels  360 us (100%)
    pallas_call x1, Pallas kernels, pair_sum(): pl.pallas_call(functools.partial(pair_kernel, n_seq), out_shape=(shape((b...  107 us
    pallas_call x1, Pallas kernels, final_sum(): pl.pallas_call(functools.partial(final_kernel, n_seq, n_fsdp), out_shape=...  78.8 us
    pallas_call x1, Pallas kernels, mixer_forward(): pl.pallas_call(functools.partial(mixer_kernel, n_seq), out_shape=(shape((...  76.3 us
    pallas_call x1, Pallas kernels, down_sum(): pl.pallas_call(functools.partial(down_kernel, n_seq), out_shape=(shape((r...  56.6 us
    pallas_call x1, Pallas kernels, glu(): pl.pallas_call(functools.partial(glu_kernel, n_seq), out_shape=(half, hal...  34.8 us

commit v1 on v0

--- a/solution.py
+++ b/solution.py
@@ -1030,17 +1030,15 @@
     core = s % 2
     mate = (s + 1 - 2 * core, f)
     links, local = Links(send, recv), Locals(local_sems)
+    loads = [local.start(w_down, wd), local.start(cot_all, cot_ref)]
+    two_ref[:rows] = two[...]
+    enter([(s, fx), (s, fy), mate])
+    own = gather_start(links, two_ref, two_ref, rows, s, fx, fy)
+    wait_all(loads)
     loads = [
-        local.start(w_down, wd),
-        local.start(cot_all, cot_ref),
         local.start(w_gate, wv.at[:, pl.ds(0, units)]),
         local.start(w_up, wv.at[:, pl.ds(units, units)]),
     ]
-    two_ref[:rows] = two[...]
-    enter([(s, fx), (s, fy), mate])
-    own = gather_start(links, two_ref, two_ref, rows, s, fx, fy)
-    loads[0].wait()
-    loads[1].wait()
     swaps, stays = swap_columns(links, local, cot_ref, cot_half, n_seq, core, mate)
 
     def act_tile(n, _):
@@ -1053,8 +1051,7 @@
         rest = slice(units // 256 * 256, units)
         d_act[:, rest] = mm_t(cot_ref[...], wd[rest])
     later = gather_forward(links, own, two_ref, rows, s, fx, fy)
-    loads[2].wait()
-    loads[3].wait()
+    wait_all(loads)
 
     def slots(first, number):
         nonlocal swaps, stays
@@ -1079,11 +1076,13 @@
             d_up[to] = (d * silu).astype(BF16)
             return 0
 
-        lax.fori_loop(0, number * rows // 16, rows_of, 0)
-        at = pl.ds(base, number * rows)
-        for src, dst in ((act, act_pair), (d_gate, gate_pair), (d_up, up_pair)):
-            sent, stayed = swap_rows(links, local, src, dst, at, mate)
-            swaps, stays = swaps + [sent], stays + [stayed]
+        cuts = number * rows // 2
+        for first_row in (0, cuts):
+            lax.fori_loop(first_row // 16, (first_row + cuts) // 16, rows_of, 0)
+            at = pl.ds(base + first_row, cuts)
+            for src, dst in ((act, act_pair), (d_gate, gate_pair), (d_up, up_pair)):
+                sent, stayed = swap_rows(links, local, src, dst, at, mate)
+                swaps, stays = swaps + [sent], stays + [stayed]
 
     slots(0, 1)
     gather_middle(own)
@@ -1103,7 +1102,7 @@
     shape = jax.ShapeDtypeStruct
     half = shape((2, tokens, width // 2), BF16)
     pair = shape((2, tokens, units), BF16)
-    remote_count = 6 + n_seq + 9
+    remote_count = 6 + n_seq + 18
     return pl.pallas_call(
         functools.partial(glu_kernel, n_seq),
         out_shape=(half, half, pair, pair, pair),
@@ -1121,7 +1120,7 @@
             pltpu.VMEM((tokens, units), BF16),
             pltpu.SemaphoreType.DMA((remote_count,)),
             pltpu.SemaphoreType.DMA((remote_count,)),
-            pltpu.SemaphoreType.DMA((4 + n_seq + 9,)),
+            pltpu.SemaphoreType.DMA((4 + n_seq + 18,)),
         ],
         compiler_params=params(collective_id),
         name="glu",
@@ -1178,8 +1177,8 @@
     def nth(self, i):
         return jnp.where(self.z < self.nz // 2, self.nz - 1 - i, i)
 
-    def load(self, local, src):
-        order = [self.rows(self.nth(i)) for i in range(self.nz)]
+    def load(self, local, src, first, last):
+        order = [self.rows(self.nth(i)) for i in range(first, last)]
         return [local.start(src.at[at], self.part.at[at]) for at in order]
 
     def feed_first(self):
@@ -1292,9 +1291,10 @@
     up_pair,
     w_gate,
     w_up,
-    d_two,
+    d_two_out,
     pair_part,
     down_out,
+    d_two,
     cot_ref,
     act_ref,
     two_ref,
@@ -1329,7 +1329,7 @@
         (up_pair, up_ref),
         (two_half, two_ref),
     )
-    loads = [local.start(src, dst) for src, dst in moves]
+    loads = [local.start(src, dst) for src, dst in moves[:2]]
     enter([(s, fx), (s, fy)] + z_peers(n_seq))
 
     def store(j, value):
@@ -1342,8 +1342,8 @@
 
     z_sum = ZLine(part, buf, line, n_seq, 128, 3, 11, store, leave)
     block = z_sum.block
-    loads[0].wait()
-    loads[1].wait()
+    wait_all(loads)
+    loads = [local.start(src, dst) for src, dst in moves[2:]]
 
     def down_tile(i, _):
         t = z_sum.nth(i)
@@ -1353,8 +1353,7 @@
     down_tile(jnp.int32(0), 0)
     z_sum.feed_first()
     lax.fori_loop(1, z_sum.nz, down_tile, 0)
-    for copy in loads[2:]:
-        copy.wait()
+    wait_all(loads)
 
     def two_part(first, slots, base):
         at = slice(first * rows, (first + slots) * rows)
@@ -1398,10 +1397,11 @@
     half = rows // 2
     d_two[:half] = rows_part[:half].astype(F32) + from_x[1].astype(F32) + from_y[2].astype(F32)
     d_two[half:] = rows_part[half:rows].astype(F32) + from_y[1].astype(F32) + from_x[2].astype(F32)
+    early = local.start(d_two, d_two_out)
     z_sum.serve_range(served, z_sum.calls, True)
     z_sum.drain()
     sends_done(far, near, passed)
-    stay.wait()
+    wait_all([stay, early])
 
 
 def down_sum(cot_half, act_pair, two_half, gate_pair, up_pair, w_gate, w_up, collective_id):
@@ -1421,8 +1421,9 @@
             shape((units, block), F32),
         ),
         in_specs=[ANY] * 7,
-        out_specs=(VMEM, ANY, ANY),
+        out_specs=(ANY, ANY, ANY),
         scratch_shapes=[
+            pltpu.VMEM((rows, width), F32),
             pltpu.VMEM((tokens, own), BF16),
             pltpu.VMEM((tokens, units), BF16),
             pltpu.VMEM((tokens, own), BF16),
@@ -1441,7 +1442,7 @@
             pltpu.VMEM((units, block), F32),
             pltpu.SemaphoreType.DMA((6,)),
             pltpu.SemaphoreType.DMA((6,)),
-            pltpu.SemaphoreType.DMA((8,)),
+            pltpu.SemaphoreType.DMA((9,)),
         ]
         + line_sems(n_seq, units, 128),
         compiler_params=params(collective_id),
@@ -1541,9 +1542,13 @@
         copy = pltpu.make_async_copy(pair_ref.at[:, at], pair_grad.at[:, at], line[4].at[j])
         start_or_wait(copy, start)
 
-    z_sum = ZLine(part, buf, line, n_seq, 256, 2, 11, store, leave)
-    blocks_in = z_sum.load(local, pair_part)
+    z_sum = ZLine(part, buf, line, n_seq, 256, 2, 7, store, leave)
+    blocks_in = z_sum.load(local, pair_part, 0, 1)
     rows_in = [local.start(d_two, d_middle), local.start(middle, d_normed)]
+    enter([(s, fx), (s, fy), (s, fd)] + seq_peers(n_seq))
+    blocks_in[0].wait()
+    z_sum.feed_first()
+    blocks_in = z_sum.load(local, pair_part, 1, z_sum.nz)
     loads = [local.start(w_out, wo)]
     loads += [
         local.start(src, dst)
@@ -1560,9 +1565,6 @@
         local.start(w, wv.at[:, pl.ds(i * chans, chans)]) for i, w in enumerate((w_in, w_fg, w_gt))
     ]
     weights.append(local.start(normed_half, normed_ref))
-    enter([(s, fx), (s, fy), (s, fd)] + seq_peers(n_seq))
-    blocks_in[0].wait()
-    z_sum.feed_first()
     served = 0
 
     def serve(number):
@@ -1571,7 +1573,7 @@
         served += number
 
     d_glu_gain[...] = jnp.zeros_like(d_glu_gain)
-    wait_all(rows_in, blocks_in[1:])
+    wait_all(rows_in, blocks_in)
 
     def middle_rows(i, _):
         at = pl.ds(pl.multiple_of(i * 16, 16), 16)
@@ -1862,24 +1864,29 @@
 def final_kernel(
     n_seq,
     n_fsdp,
-    d_normed,
-    d_middle,
     hidden,
-    middle,
     norm_gain,
     d_glu_gain,
     d_gain,
     d_bounds,
     table,
+    d_normed_in,
+    d_middle_in,
+    middle_in,
     mixer_part,
     act_pair,
     w_down,
-    output,
-    d_hidden,
+    output_out,
+    d_hidden_out,
     out_grad,
     rest_grad,
     sums,
     d_table,
+    d_normed,
+    d_middle,
+    middle,
+    output,
+    d_hidden,
     out_ref,
     rest_ref,
     part,
@@ -1903,7 +1910,7 @@
     local_sems,
     *line,
 ):
-    rows, width = middle.shape
+    rows, width = hidden.shape
     chans = d_gain.shape[1]
     tokens = 4 * rows
     s, f, fx, fy, fd = plane()
@@ -1932,17 +1939,19 @@
             copy = pltpu.make_async_copy(rest_ref.at[:, at], rest_grad.at[:, at], line[4].at[j])
             start_or_wait(copy, start)
 
-    z_sum = ZLine(part, buf, line, n_seq, 256, 2, 8, store, leave)
-    blocks_in = z_sum.load(local, mixer_part)
-    loads = [
-        local.start(act_pair.at[pl.ds(0, tokens)], act),
-        local.start(w_down, wd),
-    ]
+    z_sum = ZLine(part, buf, line, n_seq, 256, 2, 6, store, leave)
+    blocks_in = z_sum.load(local, mixer_part, 0, 1)
     along = seq_peers(n_seq)
     across = [(s, fx), (s, fy), (s, fd)]
     enter(across + along)
     blocks_in[0].wait()
     z_sum.feed_first()
+    loads = [local.start(act_pair.at[pl.ds(0, tokens)], act), local.start(w_down, wd)]
+    blocks_in = z_sum.load(local, mixer_part, 1, z_sum.nz)
+    rows_in = [
+        local.start(src, dst)
+        for src, dst in ((d_normed_in, d_normed), (d_middle_in, d_middle), (middle_in, middle))
+    ]
     served = 0
 
     def serve(number):
@@ -1962,7 +1971,7 @@
         norm_sum[...] += jnp.sum(came * value * scale, 0, keepdims=True)
         return 0
 
-    wait_all(blocks_in[1:], loads)
+    wait_all(loads)
 
     def glu_part(first, slots):
         at = slice(first * rows, (first + slots) * rows)
@@ -1979,6 +1988,7 @@
     glu_part(1, 2)
     near = reduce_start_near(links, rows_part, from_x, from_y, rows, s, fx, fy)
     glu_part(0, 1)
+    wait_all(blocks_in, rows_in)
     serve(2)
     lax.fori_loop(0, rows // 16, hidden_rows, 0)
     terms[...] = jnp.zeros_like(terms)
@@ -2003,12 +2013,6 @@
         terms_q[first + 3 : first + 4] = d_bounds[:, cols]
     seq_copies = [links.start(terms_q, over_seq.at[k], peer) for k, peer in enumerate(along)]
     serve(1)
-    total = terms_q[...]
-    for k, copy in enumerate(seq_copies):
-        copy.wait_recv()
-        total = total + over_seq[k]
-    along_sum[...] = total
-    fsdp_copies = [links.start(along_sum, over_fsdp.at[k], peer) for k, peer in enumerate(across)]
     serve(2)
     for copy in near + passed:
         copy.wait_recv()
@@ -2020,7 +2024,13 @@
         at = slice(first, first + middle_half)
         added = rows_part[at].astype(F32) + one[...].astype(F32) + other[...].astype(F32)
         output[at] = (middle[at] + added).astype(BF16)
-    serve(1)
+    total = terms_q[...]
+    for k, copy in enumerate(seq_copies):
+        copy.wait_recv()
+        total = total + over_seq[k]
+    along_sum[...] = total
+    fsdp_copies = [links.start(along_sum, over_fsdp.at[k], peer) for k, peer in enumerate(across)]
+    serve(2)
     for copy in fsdp_copies:
         copy.wait_recv()
     for k, group in enumerate((f, fx, fy, fd)):
@@ -2034,14 +2044,16 @@
     chosen = jnp.where((row >= 1) & (row <= LAYER), 1.0, 0.0)
     bound = jnp.sum(soft * chosen, 0, keepdims=True)
     d_table[...] = soft * (chosen - bound) * sums[3:4]
+    outs = [local.start(output, output_out), local.start(d_hidden, d_hidden_out)]
     z_sum.serve_range(served, z_sum.calls, True)
     z_sum.drain()
+    wait_all(outs)
     sends_done(far, near, passed, quarter_copies, seq_copies, fsdp_copies)
 
 
-def final_sum(rows_in, gains, table, mixer_part, act_pair, w_down, cid):
+def final_sum(hidden, rows_in, gains, table, mixer_part, act_pair, w_down, cid):
     n_seq, n_fsdp = lax.axis_size("seq"), lax.axis_size("fsdp")
-    rows, width = rows_in[0].shape
+    rows, width = hidden.shape
     own, columns = mixer_part.shape
     units = w_down.shape[0]
     chans = columns // 4
@@ -2061,9 +2073,14 @@
             shape((4, width), F32),
             shape(table.shape, F32),
         ),
-        in_specs=[VMEM] * 9 + [ANY] * 3,
-        out_specs=(VMEM, VMEM, ANY, ANY, VMEM, VMEM),
+        in_specs=[VMEM] * 6 + [ANY] * 6,
+        out_specs=(ANY,) * 4 + (VMEM,) * 2,
         scratch_shapes=[
+            pltpu.VMEM((rows, width), F32),
+            pltpu.VMEM((rows, width), F32),
+            pltpu.VMEM((rows, width), F32),
+            pltpu.VMEM((rows, width), BF16),
+            pltpu.VMEM((rows, width), BF16),
             pltpu.VMEM((chans, block), F32),
             pltpu.VMEM((block, 3 * chans), F32),
             pltpu.VMEM((own, columns), BF16),
@@ -2084,12 +2101,12 @@
             pltpu.VMEM((n_fsdp - 1,) + terms, F32),
             pltpu.SemaphoreType.DMA((count,)),
             pltpu.SemaphoreType.DMA((count,)),
-            pltpu.SemaphoreType.DMA((2 + n_seq // 2,)),
+            pltpu.SemaphoreType.DMA((7 + n_seq // 2,)),
         ]
         + line_sems(n_seq, columns, 256),
         compiler_params=params(cid),
         name="final_sum",
-    )(*rows_in, *gains, table, mixer_part, act_pair, w_down)
+    )(hidden, *gains, table, *rows_in, mixer_part, act_pair, w_down)
 
 
 def hand_over_kernel(count, pieces, *refs):
@@ -2193,7 +2210,8 @@
         3,
     )
     output, d_hidden, out_grad, rest_grad, sums, d_table = final_sum(
-        (d_normed, d_middle, hidden, middle),
+        hidden,
+        (d_normed, d_middle, middle),
         (gains[0], d_glu_gain, d_gain, d_bounds),
         lower_table,
         mixer_part,

time: 361 us -> 355 us (0.983)
  Pallas kernels: 360 us -> 354 us
where the time goes in v1:
time: 355 us
  Pallas kernels  354 us (100%)
    pallas_call x1, Pallas kernels, pair_sum(): pl.pallas_call(functools.partial(pair_kernel, n_seq), out_shape=(shape((b...  104 us
    pallas_call x1, Pallas kernels, final_sum(): pl.pallas_call(functools.partial(final_kernel, n_seq, n_fsdp), out_shape=...  77 us
    pallas_call x1, Pallas kernels, mixer_forward(): pl.pallas_call(functools.partial(mixer_kernel, n_seq), out_shape=(shape((...  76.3 us
    pallas_call x1, Pallas kernels, down_sum(): pl.pallas_call(functools.partial(down_kernel, n_seq), out_shape=(shape((r...  55.5 us
    pallas_call x1, Pallas kernels, glu(): pl.pallas_call(functools.partial(glu_kernel, n_seq), out_shape=(half, hal...  34.6 us

profile of v1, /device:TPU:8, one launch (start us, length us, event | category | flops | bytes accessed | tf_op | source)
XLA Modules:
  0.0 355.1 jit_solution(5740775942408089090)
XLA Ops:
  0.6 76.3 %mixer_forward.1 = (bf16[2,640,1024]{2,1,0:T(8,128)(2,1)}, bf16[640,2048]{1,0:T(8,128)(2,1)}, bf16[4,160,512]{2,1,0:T(8,128)(2,1)}, bf16[4,160,512]{2,1,0:T(8,12...) custom-call(s32[4,4]{1,0:T(4,128)} %lengths.3, ...), custom_call_target="tpu_custom_call" | custom-call | tf_op jit(solution)/shard_map/mixer_forward/pallas_call | solution.py:928
  76.9 34.6 %glu.1 = (bf16[2,640,1024]{2,1,0:T(8,128)(2,1)}, bf16[2,640,1024]{2,1,0:T(8,128)(2,1)}, bf16[2,640,1408]{2,1,0:T(8,128)(2,1)}, bf16[2,640,1408]{2,1,0:T(8,128)(2,1)}, bf16[2,640,1408]{2,1,0:T(8,128)(2,1)}) custom-call(bf16[160,2048]{1,0:T(8,128)(2,1)} %get-tuple-element.55.two, bf16[640,2048]{1,0:T(8,128)(2,1)} %get-tuple-element.56.cot_all, ...), custom_call_target="tpu_custom_call" | custom-call | tf_op jit(solution)/shard_map/glu/pallas_call | solution.py:1106
  111.5 55.5 %down_sum.1 = (f32[160,2048]{1,0:T(8,128)}, bf16[1024,2816]{1,0:T(8,128)(2,1)}, f32[1408,256]{1,0:T(8,128)}) custom-call(bf16[1280,1024]{1,0:T(8,128)(2,1)} %bitcast.27, bf16[1280,1408]{1,0:T(8,128)(2,1)} %bitcast.16, bf16[1280,1024]{1,0:T(8,128)(2,1)} %bitcast.26, bf16[1280,1408]{1,0:T(8,128)(2,1)} %bitcast.21, bf16[1280,1408]{1,0:T(8,128)(2,1)} %bitcast.22, ...), custom_call_target="tpu_custom_call" | custom-call | tf_op jit(solution)/shard_map/down_sum/pallas_call | solution.py:1416
  167.0 103.9 %pair_sum.1 = (f32[256,2816]{1,0:T(8,128)}, bf16[1024,2048]{1,0:T(8,128)(2,1)}, f32[160,2048]{1,0:T(8,128)}, f32[160,2048]{1,0:T(8,128)}, f32[1,2048]{1,0:T(1,128)}, /*index=5*/f32[1,512]{1,0:T(1,128)}, f32[1,512]{1,0:T(1,128)}) custom-call(s32[4,4]{1,0:T(4,128)} %lengths.3, bf16[160,2048]{1,0:T(8,128)(2,1)} %bitcast.19, bf16[160,2048]{1,0:T(8,128)(2,1)} %bitcast.24, ...), custom_call_target="tpu_custom_call" | custom-call | tf_op jit(solution)/shard_map/pair_sum/pallas_call | solution.py:1793
  270.9 77.0 %final_sum.1 = (bf16[160,2048]{1,0:T(8,128)(2,1)}, bf16[160,2048]{1,0:T(8,128)(2,1)}, f32[512,256]{1,0:T(8,128)}, f32[256,1536]{1,0:T(8,128)}, f32[4,2048]{1,0:T(4,128)}, /*index=5*/f32[24,2048]{1,0:T(8,128)}) custom-call(bf16[160,2048]{1,0:T(8,128)(2,1)} %bitcast.20, f32[1,2048]{1,0:T(1,128)} %bitcast.33, f32[1,2048]{1,0:T(1,128)} %get-tuple-element.75.d_glu_gain, ...), custom_call_target="tpu_custom_call" | custom-call | tf_op jit(solution)/shard_map/final_sum/pallas_call | solution.py:2066
  347.9 0.0 copy-start
  347.9 6.6 %hand_over.1 = (f32[1408,256]{1,0:T(8,128)}, f32[256,1408]{1,0:T(8,128)}, f32[256,1408]{1,0:T(8,128)}, bf16[160,2048]{1,0:T(8,128)(2,1)}, bf16[160,2048]{1,0:T(8...) custom-call(f32[1408,256]{1,0:T(8,128)} %get-tuple-element.62.refs_0, ...), custom_call_target="tpu_custom_call" | custom-call | tf_op jit(solution)/shard_map/hand_over/pallas_call | solution.py:2138
  354.5 0.0 copy-done
  354.5 0.6 fusion
Async XLA Ops:
  347.9 6.6 %copy-start = (f32[4,2048]{1,0:T(4,128)S(1)}, f32[4,2048]{1,0:T(4,128)}, u32[]{:S(2)}) copy-start(f32[4,2048]{1,0:T(4,128)} %get-tuple-element.92) | copy-start | bytes 98308

commit v2 on v1

--- a/solution.py
+++ b/solution.py
@@ -994,11 +994,6 @@
     return copies, stays
 
 
-def swap_rows(links, local, src, dst, at, mate):
-    copy = links.start(src.at[at], dst.at[1, at], mate)
-    return copy, local.start(src.at[at], dst.at[0, at])
-
-
 def glu_kernel(
     n_seq,
     two,
@@ -1053,7 +1048,7 @@
     later = gather_forward(links, own, two_ref, rows, s, fx, fy)
     wait_all(loads)
 
-    def slots(first, number):
+    def slots(first, number, swap=True):
         nonlocal swaps, stays
         base = first * rows
 
@@ -1081,15 +1076,16 @@
             lax.fori_loop(first_row // 16, (first_row + cuts) // 16, rows_of, 0)
             at = pl.ds(base + first_row, cuts)
             for src, dst in ((act, act_pair), (d_gate, gate_pair), (d_up, up_pair)):
-                sent, stayed = swap_rows(links, local, src, dst, at, mate)
-                swaps, stays = swaps + [sent], stays + [stayed]
+                stays = stays + [local.start(src.at[at], dst.at[0, at])]
+                if swap:
+                    swaps = swaps + [links.start(src.at[at], dst.at[1, at], mate)]
 
     slots(0, 1)
     gather_middle(own)
     slots(1, 2)
     gather_far(later)
     more, keeps = swap_columns(links, local, two_ref, two_half, n_seq, core, mate)
-    slots(3, 1)
+    slots(3, 1, False)
     sends_done(own, later)
     wait_all(swaps, stays, more, keeps)
 
@@ -1102,7 +1098,7 @@
     shape = jax.ShapeDtypeStruct
     half = shape((2, tokens, width // 2), BF16)
     pair = shape((2, tokens, units), BF16)
-    remote_count = 6 + n_seq + 18
+    remote_count = 6 + n_seq + 12
     return pl.pallas_call(
         functools.partial(glu_kernel, n_seq),
         out_shape=(half, half, pair, pair, pair),
@@ -1320,17 +1316,14 @@
     units = act_pair.shape[1]
     s, f, fx, fy, fd = plane()
     links, local = Links(send, recv), Locals(local_sems)
-    moves = (
-        (cot_half, cot_ref),
-        (act_pair, act_ref),
-        (w_gate, wg),
-        (w_up, wu),
-        (gate_pair, gate_ref),
-        (up_pair, up_ref),
-        (two_half, two_ref),
-    )
-    loads = [local.start(src, dst) for src, dst in moves[:2]]
-    enter([(s, fx), (s, fy)] + z_peers(n_seq))
+    core = s % 2
+    mate = (s + 1 - 2 * core, f)
+    tokens = 4 * rows
+    near_rows, far_own = pl.ds(0, 2 * tokens - rows), pl.ds(3 * rows, rows)
+    far_mate = pl.ds(2 * tokens - rows, rows)
+    loads = [local.start(act_pair.at[near_rows], act_ref.at[near_rows])]
+    enter([(s, fx), (s, fy), mate] + z_peers(n_seq))
+    swaps = [links.start(act_pair.at[far_own], act_ref.at[far_mate], mate)]
 
     def store(j, value):
         down_ref[tile(j, 128)] = value.T
@@ -1342,8 +1335,26 @@
 
     z_sum = ZLine(part, buf, line, n_seq, 128, 3, 11, store, leave)
     block = z_sum.block
-    wait_all(loads)
-    loads = [local.start(src, dst) for src, dst in moves[2:]]
+    tiles_in = [
+        local.start(cot_half.at[:, at], cot_ref.at[:, at])
+        for at in (tile(z_sum.nth(i), block) for i in range(z_sum.nz))
+    ]
+    wait_all(loads, tiles_in[:1])
+    swaps[0].wait_recv()
+    swaps += [
+        links.start(src.at[far_own], dst.at[far_mate], mate)
+        for src, dst in ((gate_pair, gate_ref), (up_pair, up_ref))
+    ]
+    loads = [
+        local.start(src, dst)
+        for src, dst in (
+            (w_gate, wg),
+            (w_up, wu),
+            (gate_pair.at[near_rows], gate_ref.at[near_rows]),
+            (up_pair.at[near_rows], up_ref.at[near_rows]),
+            (two_half, two_ref),
+        )
+    ]
 
     def down_tile(i, _):
         t = z_sum.nth(i)
@@ -1352,8 +1363,11 @@
 
     down_tile(jnp.int32(0), 0)
     z_sum.feed_first()
+    wait_all(tiles_in[1:])
     lax.fori_loop(1, z_sum.nz, down_tile, 0)
     wait_all(loads)
+    for copy in swaps[1:]:
+        copy.wait_recv()
 
     def two_part(first, slots, base):
         at = slice(first * rows, (first + slots) * rows)
@@ -1400,7 +1414,7 @@
     early = local.start(d_two, d_two_out)
     z_sum.serve_range(served, z_sum.calls, True)
     z_sum.drain()
-    sends_done(far, near, passed)
+    sends_done(swaps, far, near, passed)
     wait_all([stay, early])
 
 
@@ -1440,14 +1454,88 @@
             pltpu.VMEM(half, BF16),
             pltpu.VMEM((own, 2 * units), BF16),
             pltpu.VMEM((units, block), F32),
-            pltpu.SemaphoreType.DMA((6,)),
-            pltpu.SemaphoreType.DMA((6,)),
             pltpu.SemaphoreType.DMA((9,)),
+            pltpu.SemaphoreType.DMA((9,)),
+            pltpu.SemaphoreType.DMA((8 + n_seq // 2,)),
         ]
         + line_sems(n_seq, units, 128),
         compiler_params=params(collective_id),
         name="down_sum",
     )(cot_half, act_pair, two_half, gate_pair, up_pair, w_gate, w_up)
+
+
+class TotalsFromAbove:
+    def __init__(self, total, gathered, send, recv, n_seq):
+        self.total, self.gathered, self.send, self.recv = total, gathered, send, recv
+        self.s, self.f = lax.axis_index("seq"), lax.axis_index("fsdp")
+        self.nz = n_seq // 2
+        self.z, self.core = self.s // 2, self.s % 2
+        self.mate = (2 * self.z + 1 - self.core, self.f)
+
+    def down(self, sender, target):
+        return remote(
+            self.total,
+            self.gathered.at[2 * sender + self.core],
+            self.send.at[target],
+            self.recv.at[2 * sender + self.core],
+            (2 * target + self.core, self.f),
+        )
+
+    def across(self, sender, core):
+        slot = 2 * sender + core
+        return remote(
+            self.gathered.at[slot],
+            self.gathered.at[slot],
+            self.send.at[self.nz + sender],
+            self.recv.at[slot],
+            self.mate,
+        )
+
+    def to_mate(self, core):
+        slot = 2 * self.z + core
+        return remote(
+            self.total,
+            self.gathered.at[slot],
+            self.send.at[2 * self.nz],
+            self.recv.at[slot],
+            self.mate,
+        )
+
+    def start(self):
+        self.to_mate(self.core).start()
+        for target in range(self.nz - 1):
+
+            @pl.when(target < self.z)
+            def _():
+                self.down(self.z, target).start()
+
+    def relay(self):
+        for sender in range(1, self.nz):
+
+            @pl.when(sender > self.z)
+            def _():
+                self.down(sender, self.z).wait_recv()
+                self.across(sender, self.core).start()
+
+    def wait(self):
+        self.to_mate(1 - self.core).wait_recv()
+        for sender in range(1, self.nz):
+
+            @pl.when(sender > self.z)
+            def _():
+                self.across(sender, 1 - self.core).wait_recv()
+
+    def drain(self):
+        self.to_mate(self.core).wait_send()
+        for z in range(self.nz):
+
+            @pl.when(z < self.z)
+            def _():
+                self.down(self.z, z).wait_send()
+
+            @pl.when(z > self.z)
+            def _():
+                self.across(z, self.core).wait_send()
 
 
 def pair_kernel(
@@ -1677,9 +1765,12 @@
     p_all, s_all = segment_totals(end_p, end_s, blocks, range(7, -1, -1))
     total[:blocks] = p_all
     total[blocks:] = s_all
-    copies = start_exchange(total, gathered, exchange_send, exchange_recv, n_seq)
-    serve(2)
-    wait_all(copies)
+    above = TotalsFromAbove(total, gathered, exchange_send, exchange_recv, n_seq)
+    above.start()
+    serve(1)
+    above.relay()
+    serve(1)
+    above.wait()
     carry = jnp.zeros((blocks, 128), F32)
     for j in range(n_seq - 1, 0, -1):
         carry = jnp.where(j > s, gathered[j, blocks:] + gathered[j, :blocks] * carry, carry)
@@ -1770,6 +1861,7 @@
     outs.append(local.start(d_normed, d_normed_out))
     z_sum.serve_range(served, z_sum.calls, True)
     z_sum.drain()
+    above.drain()
     sends_done(own, later, dot_copies, swaps, far, near, passed)
     for t in range(z_sum.nz - 2, z_sum.nz):
         tile_out(jnp.int32(t)).wait()
@@ -1788,7 +1880,6 @@
     block = width // n_seq
     half = (rows // 2, width)
     shape = jax.ShapeDtypeStruct
-    exchange = pltpu.SemaphoreType.DMA((n_seq,))
     count = 18 + n_seq // 2
     return pl.pallas_call(
         functools.partial(pair_kernel, n_seq),
@@ -1839,8 +1930,8 @@
             pltpu.VMEM((n_seq, 2 * blocks, 128), F32),
             pltpu.SemaphoreType.DMA((count,)),
             pltpu.SemaphoreType.DMA((count,)),
-            exchange,
-            exchange,
+            pltpu.SemaphoreType.DMA((n_seq + 1,)),
+            pltpu.SemaphoreType.DMA((n_seq,)),
             pltpu.SemaphoreType.DMA((15 + n_seq // 2,)),
             pltpu.SemaphoreType.DMA((2,)),
         ]
@@ -1880,7 +1971,9 @@
     d_hidden_out,
     out_grad,
     rest_grad,
-    sums,
+    norm_out,
+    glu_out,
+    gate_out,
     d_table,
     d_normed,
     d_middle,
@@ -1899,9 +1992,12 @@
     pass_x,
     pass_y,
     norm_sum,
+    bounds_out,
     terms,
     quarters_in,
     terms_q,
+    from_mate,
+    terms_chip,
     over_seq,
     along_sum,
     over_fsdp,
@@ -2011,7 +2107,7 @@
         terms_q[first : first + 2] = quarter[:2, cols]
         terms_q[first + 2 : first + 3] = d_gain[:, cols]
         terms_q[first + 3 : first + 4] = d_bounds[:, cols]
-    seq_copies = [links.start(terms_q, over_seq.at[k], peer) for k, peer in enumerate(along)]
+    mate_copy = links.start(terms_q, from_mate, (s + 1 - 2 * (s % 2), f))
     serve(1)
     serve(2)
     for copy in near + passed:
@@ -2024,7 +2120,13 @@
         at = slice(first, first + middle_half)
         added = rows_part[at].astype(F32) + one[...].astype(F32) + other[...].astype(F32)
         output[at] = (middle[at] + added).astype(BF16)
-    total = terms_q[...]
+    mate_copy.wait_recv()
+    terms_chip[...] = terms_q[...] + from_mate[...]
+    seq_copies = [
+        links.start(terms_chip, over_seq.at[k], peer) for k, peer in enumerate(z_peers(n_seq))
+    ]
+    serve(2)
+    total = terms_chip[...]
     for k, copy in enumerate(seq_copies):
         copy.wait_recv()
         total = total + over_seq[k]
@@ -2037,18 +2139,19 @@
         total = along_sum[...] if k == 0 else over_fsdp[k - 1]
         for i in range(2):
             at = pl.ds(pl.multiple_of(group * chans + i * half, 128), half)
-            sums[:, at] = total[4 * i : 4 * i + 4]
+            for r, out in enumerate((norm_out, glu_out, gate_out, bounds_out)):
+                out[:, at] = total[4 * i + r : 4 * i + r + 1]
     powers = jnp.exp(table[...] - jnp.max(table[...], 0, keepdims=True))
     soft = powers / jnp.sum(powers, 0, keepdims=True)
     row = lax.broadcasted_iota(jnp.int32, soft.shape, 0)
     chosen = jnp.where((row >= 1) & (row <= LAYER), 1.0, 0.0)
     bound = jnp.sum(soft * chosen, 0, keepdims=True)
-    d_table[...] = soft * (chosen - bound) * sums[3:4]
+    d_table[...] = soft * (chosen - bound) * bounds_out[...]
     outs = [local.start(output, output_out), local.start(d_hidden, d_hidden_out)]
     z_sum.serve_range(served, z_sum.calls, True)
     z_sum.drain()
     wait_all(outs)
-    sends_done(far, near, passed, quarter_copies, seq_copies, fsdp_copies)
+    sends_done(far, near, passed, quarter_copies, [mate_copy], seq_copies, fsdp_copies)
 
 
 def final_sum(hidden, rows_in, gains, table, mixer_part, act_pair, w_down, cid):
@@ -2062,7 +2165,7 @@
     half = (rows // 2, width)
     terms = (8, chans // 2)
     shape = jax.ShapeDtypeStruct
-    count = 6 + n_seq - 1 + 2 * (n_fsdp - 1)
+    count = 6 + n_seq // 2 + 2 * (n_fsdp - 1)
     return pl.pallas_call(
         functools.partial(final_kernel, n_seq, n_fsdp),
         out_shape=(
@@ -2070,11 +2173,13 @@
             shape((rows, width), BF16),
             shape((chans, block), F32),
             shape((block, 3 * chans), F32),
-            shape((4, width), F32),
+            shape((1, width), F32),
+            shape((1, width), F32),
+            shape((1, width), F32),
             shape(table.shape, F32),
         ),
         in_specs=[VMEM] * 6 + [ANY] * 6,
-        out_specs=(ANY,) * 4 + (VMEM,) * 2,
+        out_specs=(ANY,) * 4 + (VMEM,) * 4,
         scratch_shapes=[
             pltpu.VMEM((rows, width), F32),
             pltpu.VMEM((rows, width), F32),
@@ -2093,10 +2198,13 @@
             pltpu.VMEM(half, BF16),
             pltpu.VMEM(half, BF16),
             pltpu.VMEM((1, width), F32),
+            pltpu.VMEM((1, width), F32),
             pltpu.VMEM((n_fsdp, 8, chans), F32),
             pltpu.VMEM((n_fsdp - 1, 8, chans), F32),
             pltpu.VMEM(terms, F32),
-            pltpu.VMEM((n_seq - 1,) + terms, F32),
+            pltpu.VMEM(terms, F32),
+            pltpu.VMEM(terms, F32),
+            pltpu.VMEM((n_seq // 2 - 1,) + terms, F32),
             pltpu.VMEM(terms, F32),
             pltpu.VMEM((n_fsdp - 1,) + terms, F32),
             pltpu.SemaphoreType.DMA((count,)),
@@ -2209,7 +2317,7 @@
         normed_half.reshape(2 * tokens, -1),
         3,
     )
-    output, d_hidden, out_grad, rest_grad, sums, d_table = final_sum(
+    output, d_hidden, out_grad, rest_grad, *sums, d_table = final_sum(
         hidden,
         (d_normed, d_middle, middle),
         (gains[0], d_glu_gain, d_gain, d_bounds),
@@ -2232,8 +2340,9 @@
         in_grad,
         fg_grad,
         gt_grad,
+        *sums,
     ) = hand_over(
-        (down_grad, pair_grad, output, d_hidden, d_table, out_grad, rest_grad),
+        (down_grad, pair_grad, output, d_hidden, d_table, out_grad, rest_grad, *sums),
         (
             (0, 0, block),
             (1, 0, units),
@@ -2245,6 +2354,9 @@
             (6, 0, chans),
             (6, chans, chans),
             (6, 2 * chans, chans),
+            (7, 0, width),
+            (8, 0, width),
+            (9, 0, width),
         ),
     )
     return (
@@ -2254,9 +2366,9 @@
         fg_grad,
         gt_grad,
         out_grad,
-        sums[0],
-        sums[2],
-        sums[1],
+        sums[0][0],
+        sums[2][0],
+        sums[1][0],
         d_table,
         gate_grad,
         up_grad,

time: 355 us -> 352 us (level)
  no operation moved by 1% of the time
where the time goes in v2:
time: 352 us
  Pallas kernels  351 us (100%)
    pallas_call x1, Pallas kernels, pair_sum(): pl.pallas_call(functools.partial(pair_kernel, n_seq), out_shape=(shape((b...  106 us
    pallas_call x1, Pallas kernels, mixer_forward(): pl.pallas_call(functools.partial(mixer_kernel, n_seq), out_shape=(shape((...  76.3 us
    pallas_call x1, Pallas kernels, final_sum(): pl.pallas_call(functools.partial(final_kernel, n_seq, n_fsdp), out_shape=...  75 us
    pallas_call x1, Pallas kernels, down_sum(): pl.pallas_call(functools.partial(down_kernel, n_seq), out_shape=(shape((r...  55.1 us
    pallas_call x1, Pallas kernels, glu(): pl.pallas_call(functools.partial(glu_kernel, n_seq), out_shape=(half, hal...  32.5 us

profile of v2, /device:TPU:8, one launch (start us, length us, event | category | flops | bytes accessed | tf_op | source)
XLA Modules:
  0.0 352.1 jit_solution(10442480830367122987)
XLA Ops:
  0.6 76.3 %mixer_forward.1 = (bf16[2,640,1024]{2,1,0:T(8,128)(2,1)}, bf16[640,2048]{1,0:T(8,128)(2,1)}, bf16[4,160,512]{2,1,0:T(8,128)(2,1)}, bf16[4,160,512]{2,1,0:T(8,12...) custom-call(s32[4,4]{1,0:T(4,128)} %lengths.3, ...), custom_call_target="tpu_custom_call" | custom-call | tf_op jit(solution)/shard_map/mixer_forward/pallas_call | solution.py:928
  77.0 32.5 %glu.1 = (bf16[2,640,1024]{2,1,0:T(8,128)(2,1)}, bf16[2,640,1024]{2,1,0:T(8,128)(2,1)}, bf16[2,640,1408]{2,1,0:T(8,128)(2,1)}, bf16[2,640,1408]{2,1,0:T(8,128)(2,1)}, bf16[2,640,1408]{2,1,0:T(8,128)(2,1)}) custom-call(bf16[160,2048]{1,0:T(8,128)(2,1)} %get-tuple-element.60.two, bf16[640,2048]{1,0:T(8,128)(2,1)} %get-tuple-element.61.cot_all, ...), custom_call_target="tpu_custom_call" | custom-call | tf_op jit(solution)/shard_map/glu/pallas_call | solution.py:1102
  109.5 55.1 %down_sum.1 = (f32[160,2048]{1,0:T(8,128)}, bf16[1024,2816]{1,0:T(8,128)(2,1)}, f32[1408,256]{1,0:T(8,128)}) custom-call(bf16[1280,1024]{1,0:T(8,128)(2,1)} %bitcast.27, bf16[1280,1408]{1,0:T(8,128)(2,1)} %bitcast.16, bf16[1280,1024]{1,0:T(8,128)(2,1)} %bitcast.26, bf16[1280,1408]{1,0:T(8,128)(2,1)} %bitcast.21, bf16[1280,1408]{1,0:T(8,128)(2,1)} %bitcast.22, ...), custom_call_target="tpu_custom_call" | custom-call | tf_op jit(solution)/shard_map/down_sum/pallas_call | solution.py:1430
  164.5 105.7 %pair_sum.1 = (f32[256,2816]{1,0:T(8,128)}, bf16[1024,2048]{1,0:T(8,128)(2,1)}, f32[160,2048]{1,0:T(8,128)}, f32[160,2048]{1,0:T(8,128)}, f32[1,2048]{1,0:T(1,128)}, /*index=5*/f32[1,512]{1,0:T(1,128)}, f32[1,512]{1,0:T(1,128)}) custom-call(s32[4,4]{1,0:T(4,128)} %lengths.3, bf16[160,2048]{1,0:T(8,128)(2,1)} %bitcast.19, bf16[160,2048]{1,0:T(8,128)(2,1)} %bitcast.24, ...), custom_call_target="tpu_custom_call" | custom-call | tf_op jit(solution)/shard_map/pair_sum/pallas_call | solution.py:1884
  270.2 75.0 %final_sum.1 = (bf16[160,2048]{1,0:T(8,128)(2,1)}, bf16[160,2048]{1,0:T(8,128)(2,1)}, f32[512,256]{1,0:T(8,128)}, f32[256,1536]{1,0:T(8,128)}, f32[1,2048]{1,0:T...) custom-call(bf16[160,2048]{1,0:T(8,128)(2,1)} %bitcast.20, f32[1,2048]{1,0:T(1,128)} %bitcast.33, ...), custom_call_target="tpu_custom_call" | custom-call | tf_op jit(solution)/shard_map/final_sum/pallas_call | solution.py:2169
  345.3 6.6 %hand_over.1 = (f32[1408,256]{1,0:T(8,128)}, f32[256,1408]{1,0:T(8,128)}, f32[256,1408]{1,0:T(8,128)}, bf16[160,2048]{1,0:T(8,128)(2,1)}, bf16[160,2048]{1,0:T(8...) custom-call(f32[1408,256]{1,0:T(8,128)} %get-tuple-element.67.refs_0, ...), custom_call_target="tpu_custom_call" | custom-call | tf_op jit(solution)/shard_map/hand_over/pallas_call | solution.py:2246

commit v3 on v2

--- a/solution.py
+++ b/solution.py
@@ -28,9 +28,9 @@
     return sigma * (1.0 + value * (1.0 - sigma))
 
 
-def params(collective_id):
+def params(collective_id, limit=56):
     return pltpu.CompilerParams(
-        collective_id=collective_id, has_side_effects=True, vmem_limit_bytes=56 << 20
+        collective_id=collective_id, has_side_effects=True, vmem_limit_bytes=limit << 20
     )
 
 
@@ -1563,8 +1563,8 @@
     normed_half,
     pair_grad,
     mixer_part,
-    d_normed_out,
-    d_middle_out,
+    rows_out,
+    sums_ref,
     d_glu_gain,
     d_gain,
     d_bounds,
@@ -1681,7 +1681,7 @@
         return 0
 
     lax.fori_loop(0, rows // 16, middle_rows, 0)
-    outs = [local.start(d_middle, d_middle_out)]
+    outs = [local.start(d_middle, rows_out.at[pl.ds(rows, rows)])]
     own = gather_start(links, mixed_all, mixed_all, rows, s, fx, fy)
     dot_copies = [
         links.start(dots.at[0], dots.at[k], (s, peer)) for k, peer in ((1, fx), (2, fy), (3, fd))
@@ -1858,7 +1858,12 @@
     d_normed[half:] = (
         rows_part[half:rows].astype(F32) + from_y[1].astype(F32) + from_x[2].astype(F32)
     )
-    outs.append(local.start(d_normed, d_normed_out))
+    outs.append(local.start(d_normed, rows_out.at[pl.ds(0, rows)]))
+    sums_ref[...] = jnp.zeros_like(sums_ref)
+    sums_ref[0:1] = d_glu_gain[...]
+    sums_ref[1:2, :chans] = d_gain[...]
+    sums_ref[2:3, :chans] = d_bounds[...]
+    outs.append(local.start(sums_ref, rows_out.at[pl.ds(2 * rows, 8)]))
     z_sum.serve_range(served, z_sum.calls, True)
     z_sum.drain()
     above.drain()
@@ -1886,15 +1891,15 @@
         out_shape=(
             shape((block, columns), F32),
             shape((own, 4 * chans), BF16),
-            shape((rows, width), F32),
-            shape((rows, width), F32),
-            shape((1, width), F32),
-            shape((1, chans), F32),
-            shape((1, chans), F32),
+            shape((2 * rows + 8, width), F32),
         ),
         in_specs=[pl.BlockSpec(memory_space=pltpu.SMEM)] + [VMEM] * 6 + [ANY] * 14,
-        out_specs=(ANY,) * 4 + (VMEM,) * 3,
+        out_specs=(ANY,) * 3,
         scratch_shapes=[
+            pltpu.VMEM((8, width), F32),
+            pltpu.VMEM((1, width), F32),
+            pltpu.VMEM((1, chans), F32),
+            pltpu.VMEM((1, chans), F32),
             pltpu.VMEM((rows, width), F32),
             pltpu.VMEM((rows, width), F32),
             pltpu.VMEM((block, columns), F32),
@@ -1932,7 +1937,7 @@
             pltpu.SemaphoreType.DMA((count,)),
             pltpu.SemaphoreType.DMA((n_seq + 1,)),
             pltpu.SemaphoreType.DMA((n_seq,)),
-            pltpu.SemaphoreType.DMA((15 + n_seq // 2,)),
+            pltpu.SemaphoreType.DMA((16 + n_seq // 2,)),
             pltpu.SemaphoreType.DMA((2,)),
         ]
         + line_sems(n_seq, columns, 256),
@@ -1957,12 +1962,8 @@
     n_fsdp,
     hidden,
     norm_gain,
-    d_glu_gain,
-    d_gain,
-    d_bounds,
     table,
-    d_normed_in,
-    d_middle_in,
+    float_rows,
     middle_in,
     mixer_part,
     act_pair,
@@ -1975,6 +1976,7 @@
     glu_out,
     gate_out,
     d_table,
+    sums_ref,
     d_normed,
     d_middle,
     middle,
@@ -2007,7 +2009,7 @@
     *line,
 ):
     rows, width = hidden.shape
-    chans = d_gain.shape[1]
+    chans = out_grad.shape[0]
     tokens = 4 * rows
     s, f, fx, fy, fd = plane()
     links, local = Links(send, recv), Locals(local_sems)
@@ -2046,7 +2048,12 @@
     blocks_in = z_sum.load(local, mixer_part, 1, z_sum.nz)
     rows_in = [
         local.start(src, dst)
-        for src, dst in ((d_normed_in, d_normed), (d_middle_in, d_middle), (middle_in, middle))
+        for src, dst in (
+            (float_rows.at[pl.ds(0, rows)], d_normed),
+            (float_rows.at[pl.ds(rows, rows)], d_middle),
+            (float_rows.at[pl.ds(2 * rows, 8)], sums_ref),
+            (middle_in, middle),
+        )
     ]
     served = 0
 
@@ -2090,7 +2097,7 @@
     terms[...] = jnp.zeros_like(terms)
     for q in range(4):
         terms[q, 0:1] = norm_sum[:, q * chans : (q + 1) * chans]
-        terms[q, 1:2] = d_glu_gain[:, q * chans : (q + 1) * chans]
+        terms[q, 1:2] = sums_ref[0:1, q * chans : (q + 1) * chans]
     quarter_copies = [
         links.start(terms.at[peer], quarters_in.at[k], (s, peer))
         for k, peer in enumerate((fx, fy, fd))
@@ -2105,8 +2112,8 @@
     half = chans // 2
     for first, cols in ((0, slice(0, half)), (4, slice(half, chans))):
         terms_q[first : first + 2] = quarter[:2, cols]
-        terms_q[first + 2 : first + 3] = d_gain[:, cols]
-        terms_q[first + 3 : first + 4] = d_bounds[:, cols]
+        terms_q[first + 2 : first + 3] = sums_ref[1:2, cols]
+        terms_q[first + 3 : first + 4] = sums_ref[2:3, cols]
     mate_copy = links.start(terms_q, from_mate, (s + 1 - 2 * (s % 2), f))
     serve(1)
     serve(2)
@@ -2154,7 +2161,7 @@
     sends_done(far, near, passed, quarter_copies, [mate_copy], seq_copies, fsdp_copies)
 
 
-def final_sum(hidden, rows_in, gains, table, mixer_part, act_pair, w_down, cid):
+def final_sum(hidden, norm_gain, table, float_rows, middle, mixer_part, act_pair, w_down, cid):
     n_seq, n_fsdp = lax.axis_size("seq"), lax.axis_size("fsdp")
     rows, width = hidden.shape
     own, columns = mixer_part.shape
@@ -2178,9 +2185,10 @@
             shape((1, width), F32),
             shape(table.shape, F32),
         ),
-        in_specs=[VMEM] * 6 + [ANY] * 6,
+        in_specs=[VMEM] * 3 + [ANY] * 5,
         out_specs=(ANY,) * 4 + (VMEM,) * 4,
         scratch_shapes=[
+            pltpu.VMEM((8, width), F32),
             pltpu.VMEM((rows, width), F32),
             pltpu.VMEM((rows, width), F32),
             pltpu.VMEM((rows, width), F32),
@@ -2209,12 +2217,12 @@
             pltpu.VMEM((n_fsdp - 1,) + terms, F32),
             pltpu.SemaphoreType.DMA((count,)),
             pltpu.SemaphoreType.DMA((count,)),
-            pltpu.SemaphoreType.DMA((7 + n_seq // 2,)),
+            pltpu.SemaphoreType.DMA((8 + n_seq // 2,)),
         ]
         + line_sems(n_seq, columns, 256),
-        compiler_params=params(cid),
+        compiler_params=params(cid, 48),
         name="final_sum",
-    )(hidden, *gains, table, *rows_in, mixer_part, act_pair, w_down)
+    )(hidden, norm_gain, table, float_rows, middle, mixer_part, act_pair, w_down)
 
 
 def hand_over_kernel(count, pieces, *refs):
@@ -2250,7 +2258,7 @@
         out_specs=(ANY,) * len(wanted),
         scratch_shapes=[pltpu.VMEM(*x) for x in shapes]
         + [pltpu.SemaphoreType.DMA((len(pieces),))] * 2,
-        compiler_params=pltpu.CompilerParams(vmem_limit_bytes=56 << 20),
+        compiler_params=pltpu.CompilerParams(vmem_limit_bytes=16 << 20),
         name="hand_over",
     )(*arrays)
 
@@ -2304,7 +2312,7 @@
         w_glu_up,
         2,
     )
-    pair_grad, mixer_part, d_normed, d_middle, d_glu_gain, d_gain, d_bounds = pair_sum(
+    pair_grad, mixer_part, float_rows = pair_sum(
         lengths,
         (hidden, cotangent),
         (gains[2], gains[1]),
@@ -2319,9 +2327,10 @@
     )
     output, d_hidden, out_grad, rest_grad, *sums, d_table = final_sum(
         hidden,
-        (d_normed, d_middle, middle),
-        (gains[0], d_glu_gain, d_gain, d_bounds),
+        gains[0],
         lower_table,
+        float_rows,
+        middle,
         mixer_part,
         act_pair.reshape(2 * tokens, -1),
         w_glu_down,

time: 352 us -> 348 us (0.989)
  Pallas kernels: 351 us -> 347 us
where the time goes in v3:
time: 348 us
  Pallas kernels  347 us (100%)
    pallas_call x1, Pallas kernels, pair_sum(): pl.pallas_call(functools.partial(pair_kernel, n_seq), out_shape=(shape((b...  105 us
    pallas_call x1, Pallas kernels, mixer_forward(): pl.pallas_call(functools.partial(mixer_kernel, n_seq), out_shape=(shape((...  76.2 us
    pallas_call x1, Pallas kernels, final_sum(): pl.pallas_call(functools.partial(final_kernel, n_seq, n_fsdp), out_shape=...  73.1 us
    pallas_call x1, Pallas kernels, down_sum(): pl.pallas_call(functools.partial(down_kernel, n_seq), out_shape=(shape((r...  55.1 us
    pallas_call x1, Pallas kernels, glu(): pl.pallas_call(functools.partial(glu_kernel, n_seq), out_shape=(half, hal...  32.5 us

profile of v3, /device:TPU:8, one launch (start us, length us, event | category | flops | bytes accessed | tf_op | source)
XLA Modules:
  0.0 348.0 jit_solution(2216031900390093919)
XLA Ops:
  0.6 76.2 %mixer_forward.1 = (bf16[2,640,1024]{2,1,0:T(8,128)(2,1)}, bf16[640,2048]{1,0:T(8,128)(2,1)}, bf16[4,160,512]{2,1,0:T(8,128)(2,1)}, bf16[4,160,512]{2,1,0:T(8,12...) custom-call(s32[4,4]{1,0:T(4,128)} %lengths.3, ...), custom_call_target="tpu_custom_call" | custom-call | tf_op jit(solution)/shard_map/mixer_forward/pallas_call | solution.py:928
  76.9 32.5 %glu.1 = (bf16[2,640,1024]{2,1,0:T(8,128)(2,1)}, bf16[2,640,1024]{2,1,0:T(8,128)(2,1)}, bf16[2,640,1408]{2,1,0:T(8,128)(2,1)}, bf16[2,640,1408]{2,1,0:T(8,128)(2,1)}, bf16[2,640,1408]{2,1,0:T(8,128)(2,1)}) custom-call(bf16[160,2048]{1,0:T(8,128)(2,1)} %get-tuple-element.56.two, bf16[640,2048]{1,0:T(8,128)(2,1)} %get-tuple-element.57.cot_all, ...), custom_call_target="tpu_custom_call" | custom-call | tf_op jit(solution)/shard_map/glu/pallas_call | solution.py:1102
  109.4 55.1 %down_sum.1 = (f32[160,2048]{1,0:T(8,128)}, bf16[1024,2816]{1,0:T(8,128)(2,1)}, f32[1408,256]{1,0:T(8,128)}) custom-call(bf16[1280,1024]{1,0:T(8,128)(2,1)} %bitcast.29, bf16[1280,1408]{1,0:T(8,128)(2,1)} %bitcast.21, bf16[1280,1024]{1,0:T(8,128)(2,1)} %bitcast.28, bf16[1280,1408]{1,0:T(8,128)(2,1)} %bitcast.23, bf16[1280,1408]{1,0:T(8,128)(2,1)} %bitcast.24, ...), custom_call_target="tpu_custom_call" | custom-call | tf_op jit(solution)/shard_map/down_sum/pallas_call | solution.py:1430
  164.5 0.0 copy-start
  164.5 0.0 copy-start.1
  164.5 0.0 copy-start.3
  164.5 0.0 copy-start.5
  164.5 105.2 %pair_sum.1 = (f32[256,2816]{1,0:T(8,128)}, bf16[1024,2048]{1,0:T(8,128)(2,1)}, f32[328,2048]{1,0:T(8,128)}) custom-call(s32[4,4]{1,0:T(4,128)} %lengths.3, bf16[160,2048]{1,0:T(8,128)(2,1)} %bitcast.17, bf16[160,2048]{1,0:T(8,128)(2,1)} %bitcast.26, f32[1,2048]{1,0:T(1,128)} %bitcast.33, f32[1,2048]{1,0:T(1,128)} %bitcast.31, f32[24,2048]{1,0:T(8,128)} %table.5, ...), custom_call_target="tpu_custom_call" | custom-call | tf_op jit(solution)/shard_map/pair_sum/pallas_call | solution.py:1889
  269.7 0.0 copy-done
  269.7 0.0 copy-done.1
  269.7 0.0 copy-done.3
  269.7 0.0 copy-done.5
  269.8 0.0 copy-start.2
  269.8 0.0 copy-start.4
  269.8 73.1 %final_sum.1 = (bf16[160,2048]{1,0:T(8,128)(2,1)S(1)}, bf16[160,2048]{1,0:T(8,128)(2,1)S(1)}, f32[512,256]{1,0:T(8,128)S(1)}, f32[256,1536]{1,0:T(8,128)S(1)}, f...) custom-call(bf16[160,2048]{1,0:T(8,128)(2,1)S(1)} %bitcast.18, ...), custom_call_target="tpu_custom_call" | custom-call | tf_op jit(solution)/shard_map/final_sum/pallas_call | solution.py:2176
  342.9 0.0 copy-done.2
  342.9 0.0 copy-done.4
  342.9 5.0 %hand_over.1 = (f32[1408,256]{1,0:T(8,128)}, f32[256,1408]{1,0:T(8,128)}, f32[256,1408]{1,0:T(8,128)}, bf16[160,2048]{1,0:T(8,128)(2,1)}, bf16[160,2048]{1,0:T(8...) custom-call(f32[1408,256]{1,0:T(8,128)S(1)} %copy-done.4, ...), custom_call_target="tpu_custom_call" | custom-call | tf_op jit(solution)/shard_map/hand_over/pallas_call | solution.py:2254
Async XLA Ops:
  164.5 105.2 %copy-start = (bf16[1,160,2048]{2,1,0:T(8,128)(2,1)S(1)}, bf16[1,160,2048]{2,1,0:T(8,128)(2,1)}, u32[]{:S(2)}) copy-start(bf16[1,160,2048]{2,1,0:T(8,128)(2,1)} %param.14) | copy-start | bytes 1966084
  164.5 105.2 %copy-start.1 = (f32[160,2048]{1,0:T(8,128)S(1)}, f32[160,2048]{1,0:T(8,128)}, u32[]{:S(2)}) copy-start(f32[160,2048]{1,0:T(8,128)} %get-tuple-element.66.middle.middle_in) | copy-start | bytes 3932164
  164.5 105.2 %copy-start.3 = (f32[24,2048]{1,0:T(8,128)S(1)}, f32[24,2048]{1,0:T(8,128)}, u32[]{:S(2)}) copy-start(f32[24,2048]{1,0:T(8,128)} %table.5) | copy-start | bytes 589828
  164.5 105.2 %copy-start.5 = (f32[2048]{0:T(1024)S(1)}, f32[2048]{0:T(1024)}, u32[]{:S(2)}) copy-start(f32[2048]{0:T(1024)} %param.20) | copy-start | bytes 24580
  269.8 73.1 %copy-start.2 = (f32[256,2816]{1,0:T(8,128)S(1)}, f32[256,2816]{1,0:T(8,128)}, u32[]{:S(2)}) copy-start(f32[256,2816]{1,0:T(8,128)} %get-tuple-element.75.refs_1_) | copy-start | bytes 8650756
  269.8 73.1 %copy-start.4 = (f32[1408,256]{1,0:T(8,128)S(1)}, f32[1408,256]{1,0:T(8,128)}, u32[]{:S(2)}) copy-start(f32[1408,256]{1,0:T(8,128)} %get-tuple-element.63.refs_0_) | copy-start | bytes 4325380

commit v4 on v3

--- a/solution.py
+++ b/solution.py
@@ -1767,9 +1767,9 @@
     total[blocks:] = s_all
     above = TotalsFromAbove(total, gathered, exchange_send, exchange_recv, n_seq)
     above.start()
-    serve(1)
+    serve(2)
     above.relay()
-    serve(1)
+    serve(2)
     above.wait()
     carry = jnp.zeros((blocks, 128), F32)
     for j in range(n_seq - 1, 0, -1):
@@ -1848,9 +1848,9 @@
 
     lax.fori_loop(0, 1, mixer_tile, 0)
     passed = reduce_pass(links, far, rows_part, from_x, from_y, pass_x, pass_y, rows, s, fx, fy)
-    serve(1)
+    serve(2)
     lax.fori_loop(1, z_sum.nz, mixer_tile, 0)
-    serve(2)
+    serve(3)
     for copy in near + passed:
         copy.wait_recv()
     half = rows // 2

time: 348 us -> 346 us (level)
  no operation moved by 1% of the time
where the time goes in v4:
time: 346 us
  Pallas kernels  345 us (100%)
    pallas_call x1, Pallas kernels, pair_sum(): pl.pallas_call(functools.partial(pair_kernel, n_seq), out_shape=(shape((b...  103 us
    pallas_call x1, Pallas kernels, mixer_forward(): pl.pallas_call(functools.partial(mixer_kernel, n_seq), out_shape=(shape((...  76.2 us
    pallas_call x1, Pallas kernels, final_sum(): pl.pallas_call(functools.partial(final_kernel, n_seq, n_fsdp), out_shape=...  73.1 us
    pallas_call x1, Pallas kernels, down_sum(): pl.pallas_call(functools.partial(down_kernel, n_seq), out_shape=(shape((r...  55.1 us
    pallas_call x1, Pallas kernels, glu(): pl.pallas_call(functools.partial(glu_kernel, n_seq), out_shape=(half, hal...  32.5 us

profile of v4, /device:TPU:8, one launch (start us, length us, event | category | flops | bytes accessed | tf_op | source)
XLA Modules:
  0.0 345.9 jit_solution(1302873363075557081)
XLA Ops:
  0.6 76.2 %mixer_forward.1 = (bf16[2,640,1024]{2,1,0:T(8,128)(2,1)}, bf16[640,2048]{1,0:T(8,128)(2,1)}, bf16[4,160,512]{2,1,0:T(8,128)(2,1)}, bf16[4,160,512]{2,1,0:T(8,12...) custom-call(s32[4,4]{1,0:T(4,128)} %lengths.3, ...), custom_call_target="tpu_custom_call" | custom-call | tf_op jit(solution)/shard_map/mixer_forward/pallas_call | solution.py:928
  76.9 32.5 %glu.1 = (bf16[2,640,1024]{2,1,0:T(8,128)(2,1)}, bf16[2,640,1024]{2,1,0:T(8,128)(2,1)}, bf16[2,640,1408]{2,1,0:T(8,128)(2,1)}, bf16[2,640,1408]{2,1,0:T(8,128)(2,1)}, bf16[2,640,1408]{2,1,0:T(8,128)(2,1)}) custom-call(bf16[160,2048]{1,0:T(8,128)(2,1)} %get-tuple-element.56.two, bf16[640,2048]{1,0:T(8,128)(2,1)} %get-tuple-element.57.cot_all, ...), custom_call_target="tpu_custom_call" | custom-call | tf_op jit(solution)/shard_map/glu/pallas_call | solution.py:1102
  109.4 55.1 %down_sum.1 = (f32[160,2048]{1,0:T(8,128)}, bf16[1024,2816]{1,0:T(8,128)(2,1)}, f32[1408,256]{1,0:T(8,128)}) custom-call(bf16[1280,1024]{1,0:T(8,128)(2,1)} %bitcast.29, bf16[1280,1408]{1,0:T(8,128)(2,1)} %bitcast.21, bf16[1280,1024]{1,0:T(8,128)(2,1)} %bitcast.28, bf16[1280,1408]{1,0:T(8,128)(2,1)} %bitcast.23, bf16[1280,1408]{1,0:T(8,128)(2,1)} %bitcast.24, ...), custom_call_target="tpu_custom_call" | custom-call | tf_op jit(solution)/shard_map/down_sum/pallas_call | solution.py:1430
  164.5 0.0 copy-start
  164.5 0.0 copy-start.1
  164.5 0.0 copy-start.3
  164.5 0.0 copy-start.5
  164.5 103.0 %pair_sum.1 = (f32[256,2816]{1,0:T(8,128)}, bf16[1024,2048]{1,0:T(8,128)(2,1)}, f32[328,2048]{1,0:T(8,128)}) custom-call(s32[4,4]{1,0:T(4,128)} %lengths.3, bf16[160,2048]{1,0:T(8,128)(2,1)} %bitcast.17, bf16[160,2048]{1,0:T(8,128)(2,1)} %bitcast.26, f32[1,2048]{1,0:T(1,128)} %bitcast.33, f32[1,2048]{1,0:T(1,128)} %bitcast.31, f32[24,2048]{1,0:T(8,128)} %table.5, ...), custom_call_target="tpu_custom_call" | custom-call | tf_op jit(solution)/shard_map/pair_sum/pallas_call | solution.py:1889
  267.6 0.0 copy-done
  267.6 0.0 copy-done.1
  267.6 0.0 copy-done.3
  267.6 0.0 copy-done.5
  267.6 0.0 copy-start.2
  267.6 0.0 copy-start.4
  267.6 73.1 %final_sum.1 = (bf16[160,2048]{1,0:T(8,128)(2,1)S(1)}, bf16[160,2048]{1,0:T(8,128)(2,1)S(1)}, f32[512,256]{1,0:T(8,128)S(1)}, f32[256,1536]{1,0:T(8,128)S(1)}, f...) custom-call(bf16[160,2048]{1,0:T(8,128)(2,1)S(1)} %bitcast.18, ...), custom_call_target="tpu_custom_call" | custom-call | tf_op jit(solution)/shard_map/final_sum/pallas_call | solution.py:2176
  340.8 0.0 copy-done.2
  340.8 0.0 copy-done.4
  340.8 5.0 %hand_over.1 = (f32[1408,256]{1,0:T(8,128)}, f32[256,1408]{1,0:T(8,128)}, f32[256,1408]{1,0:T(8,128)}, bf16[160,2048]{1,0:T(8,128)(2,1)}, bf16[160,2048]{1,0:T(8...) custom-call(f32[1408,256]{1,0:T(8,128)S(1)} %copy-done.4, ...), custom_call_target="tpu_custom_call" | custom-call | tf_op jit(solution)/shard_map/hand_over/pallas_call | solution.py:2254
Async XLA Ops:
  164.5 103.1 %copy-start = (bf16[1,160,2048]{2,1,0:T(8,128)(2,1)S(1)}, bf16[1,160,2048]{2,1,0:T(8,128)(2,1)}, u32[]{:S(2)}) copy-start(bf16[1,160,2048]{2,1,0:T(8,128)(2,1)} %param.14) | copy-start | bytes 1966084
  164.5 103.1 %copy-start.1 = (f32[160,2048]{1,0:T(8,128)S(1)}, f32[160,2048]{1,0:T(8,128)}, u32[]{:S(2)}) copy-start(f32[160,2048]{1,0:T(8,128)} %get-tuple-element.66.middle.middle_in) | copy-start | bytes 3932164
  164.5 103.1 %copy-start.3 = (f32[24,2048]{1,0:T(8,128)S(1)}, f32[24,2048]{1,0:T(8,128)}, u32[]{:S(2)}) copy-start(f32[24,2048]{1,0:T(8,128)} %table.5) | copy-start | bytes 589828
  164.5 103.1 %copy-start.5 = (f32[2048]{0:T(1024)S(1)}, f32[2048]{0:T(1024)}, u32[]{:S(2)}) copy-start(f32[2048]{0:T(1024)} %param.20) | copy-start | bytes 24580
  267.6 73.1 %copy-start.2 = (f32[256,2816]{1,0:T(8,128)S(1)}, f32[256,2816]{1,0:T(8,128)}, u32[]{:S(2)}) copy-start(f32[256,2816]{1,0:T(8,128)} %get-tuple-element.75.refs_1_) | copy-start | bytes 8650756
  267.6 73.1 %copy-start.4 = (f32[1408,256]{1,0:T(8,128)S(1)}, f32[1408,256]{1,0:T(8,128)}, u32[]{:S(2)}) copy-start(f32[1408,256]{1,0:T(8,128)} %get-tuple-element.63.refs_0_) | copy-start | bytes 4325380

commit v5 on v4

--- a/solution.py
+++ b/solution.py
@@ -2115,7 +2115,7 @@
         terms_q[first + 2 : first + 3] = sums_ref[1:2, cols]
         terms_q[first + 3 : first + 4] = sums_ref[2:3, cols]
     mate_copy = links.start(terms_q, from_mate, (s + 1 - 2 * (s % 2), f))
-    serve(1)
+    serve(3)
     serve(2)
     for copy in near + passed:
         copy.wait_recv()
@@ -2132,14 +2132,14 @@
     seq_copies = [
         links.start(terms_chip, over_seq.at[k], peer) for k, peer in enumerate(z_peers(n_seq))
     ]
-    serve(2)
+    serve(3)
     total = terms_chip[...]
     for k, copy in enumerate(seq_copies):
         copy.wait_recv()
         total = total + over_seq[k]
     along_sum[...] = total
     fsdp_copies = [links.start(along_sum, over_fsdp.at[k], peer) for k, peer in enumerate(across)]
-    serve(2)
+    serve(3)
     for copy in fsdp_copies:
         copy.wait_recv()
     for k, group in enumerate((f, fx, fy, fd)):

time: 346 us -> 346 us (level)
  no operation moved by 1% of the time
where the time goes in v5:
time: 346 us
  Pallas kernels  345 us (100%)
    pallas_call x1, Pallas kernels, pair_sum(): pl.pallas_call(functools.partial(pair_kernel, n_seq), out_shape=(shape((b...  103 us
    pallas_call x1, Pallas kernels, mixer_forward(): pl.pallas_call(functools.partial(mixer_kernel, n_seq), out_shape=(shape((...  76.2 us
    pallas_call x1, Pallas kernels, final_sum(): pl.pallas_call(functools.partial(final_kernel, n_seq, n_fsdp), out_shape=...  73.1 us
    pallas_call x1, Pallas kernels, down_sum(): pl.pallas_call(functools.partial(down_kernel, n_seq), out_shape=(shape((r...  55.1 us
    pallas_call x1, Pallas kernels, glu(): pl.pallas_call(functools.partial(glu_kernel, n_seq), out_shape=(half, hal...  32.5 us

profile of v5, /device:TPU:8, one launch (start us, length us, event | category | flops | bytes accessed | tf_op | source)
XLA Modules:
  0.0 345.9 jit_solution(9465029391869360430)
XLA Ops:
  0.6 76.2 %mixer_forward.1 = (bf16[2,640,1024]{2,1,0:T(8,128)(2,1)}, bf16[640,2048]{1,0:T(8,128)(2,1)}, bf16[4,160,512]{2,1,0:T(8,128)(2,1)}, bf16[4,160,512]{2,1,0:T(8,12...) custom-call(s32[4,4]{1,0:T(4,128)} %lengths.3, ...), custom_call_target="tpu_custom_call" | custom-call | tf_op jit(solution)/shard_map/mixer_forward/pallas_call | solution.py:928
  76.9 32.5 %glu.1 = (bf16[2,640,1024]{2,1,0:T(8,128)(2,1)}, bf16[2,640,1024]{2,1,0:T(8,128)(2,1)}, bf16[2,640,1408]{2,1,0:T(8,128)(2,1)}, bf16[2,640,1408]{2,1,0:T(8,128)(2,1)}, bf16[2,640,1408]{2,1,0:T(8,128)(2,1)}) custom-call(bf16[160,2048]{1,0:T(8,128)(2,1)} %get-tuple-element.56.two, bf16[640,2048]{1,0:T(8,128)(2,1)} %get-tuple-element.57.cot_all, ...), custom_call_target="tpu_custom_call" | custom-call | tf_op jit(solution)/shard_map/glu/pallas_call | solution.py:1102
  109.4 55.1 %down_sum.1 = (f32[160,2048]{1,0:T(8,128)}, bf16[1024,2816]{1,0:T(8,128)(2,1)}, f32[1408,256]{1,0:T(8,128)}) custom-call(bf16[1280,1024]{1,0:T(8,128)(2,1)} %bitcast.29, bf16[1280,1408]{1,0:T(8,128)(2,1)} %bitcast.21, bf16[1280,1024]{1,0:T(8,128)(2,1)} %bitcast.28, bf16[1280,1408]{1,0:T(8,128)(2,1)} %bitcast.23, bf16[1280,1408]{1,0:T(8,128)(2,1)} %bitcast.24, ...), custom_call_target="tpu_custom_call" | custom-call | tf_op jit(solution)/shard_map/down_sum/pallas_call | solution.py:1430
  164.5 0.0 copy-start
  164.5 0.0 copy-start.1
  164.5 0.0 copy-start.3
  164.5 0.0 copy-start.5
  164.5 103.0 %pair_sum.1 = (f32[256,2816]{1,0:T(8,128)}, bf16[1024,2048]{1,0:T(8,128)(2,1)}, f32[328,2048]{1,0:T(8,128)}) custom-call(s32[4,4]{1,0:T(4,128)} %lengths.3, bf16[160,2048]{1,0:T(8,128)(2,1)} %bitcast.17, bf16[160,2048]{1,0:T(8,128)(2,1)} %bitcast.26, f32[1,2048]{1,0:T(1,128)} %bitcast.33, f32[1,2048]{1,0:T(1,128)} %bitcast.31, f32[24,2048]{1,0:T(8,128)} %table.5, ...), custom_call_target="tpu_custom_call" | custom-call | tf_op jit(solution)/shard_map/pair_sum/pallas_call | solution.py:1889
  267.6 0.0 copy-done
  267.6 0.0 copy-done.1
  267.6 0.0 copy-done.3
  267.6 0.0 copy-done.5
  267.6 0.0 copy-start.2
  267.6 0.0 copy-start.4
  267.6 73.1 %final_sum.1 = (bf16[160,2048]{1,0:T(8,128)(2,1)S(1)}, bf16[160,2048]{1,0:T(8,128)(2,1)S(1)}, f32[512,256]{1,0:T(8,128)S(1)}, f32[256,1536]{1,0:T(8,128)S(1)}, f...) custom-call(bf16[160,2048]{1,0:T(8,128)(2,1)S(1)} %bitcast.18, ...), custom_call_target="tpu_custom_call" | custom-call | tf_op jit(solution)/shard_map/final_sum/pallas_call | solution.py:2176
  340.8 0.0 copy-done.2
  340.8 0.0 copy-done.4
  340.8 5.0 %hand_over.1 = (f32[1408,256]{1,0:T(8,128)}, f32[256,1408]{1,0:T(8,128)}, f32[256,1408]{1,0:T(8,128)}, bf16[160,2048]{1,0:T(8,128)(2,1)}, bf16[160,2048]{1,0:T(8...) custom-call(f32[1408,256]{1,0:T(8,128)S(1)} %copy-done.4, ...), custom_call_target="tpu_custom_call" | custom-call | tf_op jit(solution)/shard_map/hand_over/pallas_call | solution.py:2254
Async XLA Ops:
  164.5 103.1 %copy-start = (bf16[1,160,2048]{2,1,0:T(8,128)(2,1)S(1)}, bf16[1,160,2048]{2,1,0:T(8,128)(2,1)}, u32[]{:S(2)}) copy-start(bf16[1,160,2048]{2,1,0:T(8,128)(2,1)} %param.14) | copy-start | bytes 1966084
  164.5 103.1 %copy-start.1 = (f32[160,2048]{1,0:T(8,128)S(1)}, f32[160,2048]{1,0:T(8,128)}, u32[]{:S(2)}) copy-start(f32[160,2048]{1,0:T(8,128)} %get-tuple-element.66.middle.middle_in) | copy-start | bytes 3932164
  164.5 103.1 %copy-start.3 = (f32[24,2048]{1,0:T(8,128)S(1)}, f32[24,2048]{1,0:T(8,128)}, u32[]{:S(2)}) copy-start(f32[24,2048]{1,0:T(8,128)} %table.5) | copy-start | bytes 589828
  164.5 103.1 %copy-start.5 = (f32[2048]{0:T(1024)S(1)}, f32[2048]{0:T(1024)}, u32[]{:S(2)}) copy-start(f32[2048]{0:T(1024)} %param.20) | copy-start | bytes 24580
  267.6 73.1 %copy-start.2 = (f32[256,2816]{1,0:T(8,128)S(1)}, f32[256,2816]{1,0:T(8,128)}, u32[]{:S(2)}) copy-start(f32[256,2816]{1,0:T(8,128)} %get-tuple-element.75.refs_1_) | copy-start | bytes 8650756
  267.6 73.1 %copy-start.4 = (f32[1408,256]{1,0:T(8,128)S(1)}, f32[1408,256]{1,0:T(8,128)}, u32[]{:S(2)}) copy-start(f32[1408,256]{1,0:T(8,128)} %get-tuple-element.63.refs_0_) | copy-start | bytes 4325380
